TPU v7x, 32 devices: a whole 2x2x4 slice. The times are simulated.
32 devices in a mesh: dp: 8 (over y, x, core), tensor: 4 (over z).
Axes of the slice: x: 2, y: 2, z: 4, core: 2. Of those that a mesh axis runs over, the one named last changes fastest.
Arguments:
- block_in: float32 [6304, 768], P(('dp', 'tensor')), may hold values from -6 to 6
- out_grad: float32 [6304, 768], P(('dp', 'tensor'))
- bank_w: float32 [4, 224, 64, 768], P('tensor', 'dp')
- bank_m: float32 [4, 224, 64, 768], P('tensor', 'dp')
- bank_v: float32 [4, 224, 64, 768], P('tensor', 'dp'), as said below
- norm_w: float32 [4, 768], replicated
- norm_m: float32 [4, 768], replicated
- norm_v: float32 [4, 768], replicated, as said below
- router_w: float32 [768, 4], replicated, may hold values from -0.14433756 to 0.14433756
- router_m: float32 [768, 4], replicated
- router_v: float32 [768, 4], replicated, as said below
- expert_ids: int32 [6304, 2], P('dp'), may hold values from 0 to 3, as said below
- fill_rank: int32 [6304, 2], P('dp'), may hold values from 0 to 1575, as said below
- owner_list: int32 [108], replicated, may hold values from 0 to 7, as said below
Outputs:
- block_out: float32 [6304, 768], P(('dp', 'tensor'))
- input_grad: float32 [6304, 768], P(('dp', 'tensor'))
- bank_first: float32 [4, 224, 64, 768], P('tensor', 'dp')
- bank_second: float32 [4, 224, 64, 768], P('tensor', 'dp')
- bank_new: float32 [4, 224, 64, 768], P('tensor', 'dp')
- norm_first: float32 [4, 768], replicated
- norm_second: float32 [4, 768], replicated
- norm_new: float32 [4, 768], replicated
- router_first: float32 [768, 4], replicated
- router_second: float32 [768, 4], replicated
- router_new: float32 [768, 4], replicated
Inputs may be any that keep to these rules, and one draw needn't show every extreme that they name: `expert_ids`: the two entries of a row differ. `fill_rank`: within each group of 788 consecutive tokens the 1576 entries name every number of 0 to 1575 once. `owner_list`: no owner is named by more than 28 tiles, and some owner by exactly 28. `bank_v`: positive. `norm_v`: positive. `router_v`: positive.
All inputs are finite; a program needn't handle non-finite values.
Results may differ from a plain program's by a relative error of at most 0.02.
Values may be sent and summed in bfloat16 or wider, within the bound.
No kernel may reach another device: no remote copies, remote signals or barrier semaphores. Data moves between devices by JAX's collectives and lax.ppermute only.
A program may use at most 192 MiB of HBM per device.

v0:
```python
import jax
import jax.numpy as jnp
from jax import lax
from jax.sharding import PartitionSpec as P

HEADS = 12
FF = 3072
SEQ = 197
EXPERTS = 4
STEP = 10
CAPACITY = 443


norm_epsilon = 1e-06
beta_first = 0.9
beta_second = 0.95
adam_epsilon = 1e-08
weight_decay = 0.1
rate_bank = 0.06
rate_norm = 0.25
rate_router = 0.05
highest = lax.Precision.HIGHEST


def layer_norm(values, gain_row, bias_row):
    center = values - jnp.mean(values, axis=-1, keepdims=True)
    variance = jnp.mean(center * center, axis=-1, keepdims=True)
    return center * lax.rsqrt(variance + norm_epsilon) * gain_row + bias_row


def adamw_update(weights, first_old, second_old, grad_total, step_rate, decay_rate):
    first_new = beta_first * first_old + (1.0 - beta_first) * grad_total
    second_new = beta_second * second_old + (1.0 - beta_second) * grad_total * grad_total
    first_hat = first_new / (1.0 - beta_first**STEP)
    second_hat = second_new / (1.0 - beta_second**STEP)
    weights_new = weights * (1.0 - step_rate * decay_rate) - step_rate * first_hat / (
        jnp.sqrt(second_hat) + adam_epsilon
    )
    return (first_new, second_new, weights_new)


def bank_positions(owner_list, owner_count, slot_width):
    owners = jnp.arange(owner_count, dtype=jnp.int32)
    member = (owner_list[:, None] == owners[None, :]).astype(jnp.int32)
    earlier = jnp.sum((jnp.cumsum(member, axis=0) - member) * member, axis=1)
    return owner_list * slot_width + earlier


def slot_table(expert_ids, fill_rank, expert_count, capacity):
    group_rows = expert_ids.shape[0]
    pair_count = 2 * group_rows
    pair_expert = expert_ids.reshape(pair_count)
    pair_rank = fill_rank.reshape(pair_count)
    pair_number = jnp.arange(pair_count, dtype=jnp.int32)
    by_rank = jnp.zeros((pair_count,), jnp.int32).at[pair_rank].set(pair_number)
    ranked_expert = pair_expert[by_rank]
    member = (ranked_expert[:, None] == jnp.arange(expert_count, dtype=jnp.int32)[None, :]).astype(
        jnp.int32
    )
    earlier = jnp.sum((jnp.cumsum(member, axis=0) - member) * member, axis=1)
    placed = earlier[pair_rank]
    slot_count = expert_count * capacity
    pair_slot = jnp.where(placed < capacity, pair_expert * capacity + placed, slot_count)
    slot_token = (
        jnp.full((slot_count + 1,), group_rows, jnp.int32).at[pair_slot].set(pair_number // 2)
    )
    return (pair_slot.reshape(group_rows, 2), slot_token[:slot_count])


def split_tiles(weight_tiles, heads_here, tile_runs, head_size):
    model_width = weight_tiles.shape[2]
    qkv_rows = weight_tiles[: 3 * heads_here].reshape(3 * heads_here * head_size, model_width)
    out_rows = weight_tiles[3 * heads_here : 4 * heads_here].reshape(
        heads_here * head_size, model_width
    )
    expert_rows = weight_tiles[4 * heads_here :].reshape(
        EXPERTS, 2, tile_runs * head_size, model_width
    )
    return (qkv_rows, out_rows, expert_rows[:, 0], expert_rows[:, 1])


def on_device(
    block_in,
    out_grad,
    bank_w,
    bank_m,
    bank_v,
    norm_w,
    norm_m,
    norm_v,
    router_w,
    router_m,
    router_v,
    expert_ids,
    fill_rank,
    owner_list,
):
    dp_count = lax.axis_size("dp")
    tensor_count = lax.axis_size("tensor")
    row_count = block_in.shape[0]
    model_width = block_in.shape[1]
    group_rows = expert_ids.shape[0]
    image_count = group_rows // SEQ
    slot_width = bank_w.shape[1]
    head_size = bank_w.shape[2]
    heads_here = HEADS // tensor_count
    tile_runs = FF // (tensor_count * head_size)
    tile_total = owner_list.shape[0]
    capacity = CAPACITY
    slot_count = EXPERTS * capacity
    positions = bank_positions(owner_list, dp_count, slot_width)
    bank_low = bank_w[0].astype(jnp.bfloat16)
    weight_tiles = lax.all_gather(bank_low, "dp", axis=0, tiled=True)[positions]
    qkv_rows, out_rows, expert_in, expert_out = split_tiles(
        weight_tiles, heads_here, tile_runs, head_size
    )
    pair_slot, slot_token = slot_table(expert_ids, fill_rank, EXPERTS, capacity)
    row_begin = lax.axis_index("tensor") * row_count
    ids_here = lax.dynamic_slice_in_dim(expert_ids, row_begin, row_count, 0)
    router_low = router_w.astype(jnp.bfloat16)
    normed_rows = layer_norm(block_in, norm_w[0], norm_w[1]).astype(jnp.bfloat16)
    normed = lax.all_gather(normed_rows, "tensor", axis=0, tiled=True)
    mixed = lax.dot_general(
        normed, qkv_rows, (((1,), (1,)), ((), ())), preferred_element_type=jnp.float32
    ).astype(jnp.bfloat16)
    mixed_parts = mixed.reshape(image_count, SEQ, 3, heads_here, head_size)
    queries = mixed_parts[:, :, 0]
    key_heads = mixed_parts[:, :, 1]
    value_heads = mixed_parts[:, :, 2]
    scale_factor = head_size ** (-0.5)
    scores = (
        jnp.einsum("bqhd,bkhd->bhqk", queries, key_heads, preferred_element_type=jnp.float32)
        * scale_factor
    )
    log_total = jax.nn.logsumexp(scores, axis=-1, keepdims=True)
    probs_low = jnp.exp(scores - log_total).astype(jnp.bfloat16)
    attended = jnp.einsum(
        "bhqk,bkhd->bqhd", probs_low, value_heads, preferred_element_type=jnp.float32
    )
    attended = attended.astype(jnp.bfloat16).reshape(group_rows, heads_here * head_size)
    branch = lax.psum_scatter(
        jnp.dot(attended, out_rows, preferred_element_type=jnp.float32).astype(jnp.bfloat16),
        "tensor",
        scatter_dimension=0,
        tiled=True,
    ).astype(jnp.float32)
    residual = block_in + branch
    second_rows = layer_norm(residual, norm_w[2], norm_w[3]).astype(jnp.bfloat16)
    second = lax.all_gather(second_rows, "tensor", axis=0, tiled=True)
    router_probs = jax.nn.softmax(
        jnp.dot(second, router_low, preferred_element_type=jnp.float32), axis=-1
    )
    gate_pair = jnp.take_along_axis(router_probs, expert_ids, axis=1)
    second_pad = jnp.concatenate([second, jnp.zeros((1, model_width), jnp.bfloat16)], axis=0)
    dispatched = second_pad[slot_token].reshape(EXPERTS, capacity, model_width)
    hidden = jnp.einsum("ecd,efd->ecf", dispatched, expert_in, preferred_element_type=jnp.float32)
    gelu_value, gelu_pull = jax.vjp(jax.nn.gelu, hidden)
    activated = gelu_value.astype(jnp.bfloat16)
    returned = jnp.einsum("ecf,efd->ecd", activated, expert_out, preferred_element_type=jnp.float32)
    returned_pad = jnp.concatenate(
        [returned.reshape(slot_count, model_width), jnp.zeros((1, model_width), jnp.float32)],
        axis=0,
    )
    block_out = residual + lax.psum_scatter(
        jnp.sum(gate_pair[:, :, None] * returned_pad[pair_slot], axis=1).astype(jnp.bfloat16),
        "tensor",
        scatter_dimension=0,
        tiled=True,
    ).astype(jnp.float32)
    back_tiles = lax.all_gather(bank_low, "dp", axis=0, tiled=True)[positions]
    qkv_back, out_back, in_back, expert_back = split_tiles(
        back_tiles, heads_here, tile_runs, head_size
    )
    grad_low = lax.all_gather(out_grad.astype(jnp.bfloat16), "tensor", axis=0, tiled=True)
    grad_pad = jnp.concatenate([grad_low, jnp.zeros((1, model_width), jnp.bfloat16)], axis=0)
    gate_part = jnp.sum(grad_low.astype(jnp.float32)[:, None, :] * returned_pad[pair_slot], axis=2)
    slot_gate = (
        jnp.zeros((slot_count + 1,), jnp.float32)
        .at[pair_slot.reshape(-1)]
        .set(gate_pair.reshape(-1))[:slot_count]
    )
    returned_grad = (slot_gate[:, None] * grad_pad[slot_token].astype(jnp.float32)).astype(
        jnp.bfloat16
    )
    returned_grad = returned_grad.reshape(EXPERTS, capacity, model_width)
    act_grad = jnp.einsum(
        "ecd,efd->ecf", returned_grad, expert_back, preferred_element_type=jnp.float32
    )
    hidden_grad = gelu_pull(act_grad)[0].astype(jnp.bfloat16)
    out_expert_grad = jnp.einsum(
        "ecf,ecd->efd", activated, returned_grad, preferred_element_type=jnp.float32
    )
    in_expert_grad = jnp.einsum(
        "ecf,ecd->efd", hidden_grad, dispatched, preferred_element_type=jnp.float32
    )
    dispatch_grad = jnp.einsum(
        "ecf,efd->ecd", hidden_grad, in_back, preferred_element_type=jnp.float32
    )
    dispatch_pad = jnp.concatenate(
        [dispatch_grad.reshape(slot_count, model_width), jnp.zeros((1, model_width), jnp.float32)],
        axis=0,
    )
    second_part = jnp.sum(dispatch_pad[pair_slot], axis=1)
    second_grad, gate_grad = (
        lax.psum_scatter(
            second_part.astype(jnp.bfloat16), "tensor", scatter_dimension=0, tiled=True
        ).astype(jnp.float32),
        lax.psum_scatter(
            gate_part.astype(jnp.bfloat16), "tensor", scatter_dimension=0, tiled=True
        ).astype(jnp.float32),
    )
    probs_here = jax.nn.softmax(
        jnp.dot(second_rows, router_low, preferred_element_type=jnp.float32), axis=-1
    )
    expert_axis = jnp.arange(EXPERTS, dtype=jnp.int32)
    probs_grad = jnp.sum(
        (ids_here[:, :, None] == expert_axis[None, None, :]).astype(jnp.float32)
        * gate_grad[:, :, None],
        axis=1,
    )
    logit_grad = probs_here * (probs_grad - jnp.sum(probs_here * probs_grad, axis=1, keepdims=True))
    router_grad = jnp.dot(second_rows.astype(jnp.float32).T, logit_grad, precision=highest)
    second_grad = second_grad + jnp.dot(
        logit_grad, router_low.astype(jnp.float32).T, precision=highest
    )
    _, second_pull = jax.vjp(layer_norm, residual, norm_w[2], norm_w[3])
    residual_part, gain_two, bias_two = second_pull(second_grad)
    residual_grad = out_grad + residual_part
    branch_low = lax.all_gather(residual_grad.astype(jnp.bfloat16), "tensor", axis=0, tiled=True)
    out_proj_grad = lax.dot_general(
        attended, branch_low, (((0,), (0,)), ((), ())), preferred_element_type=jnp.float32
    )
    attended_grad = lax.dot_general(
        branch_low, out_back, (((1,), (1,)), ((), ())), preferred_element_type=jnp.float32
    )
    attended_grad = attended_grad.astype(jnp.bfloat16).reshape(
        image_count, SEQ, heads_here, head_size
    )
    scores_again = (
        jnp.einsum("bqhd,bkhd->bhqk", queries, key_heads, preferred_element_type=jnp.float32)
        * scale_factor
    )
    probs_again = jnp.exp(scores_again - log_total)
    weight_grad = jnp.einsum(
        "bqhd,bkhd->bhqk", attended_grad, value_heads, preferred_element_type=jnp.float32
    )
    score_grad = (
        probs_again * (weight_grad - jnp.sum(probs_again * weight_grad, axis=-1, keepdims=True))
    ).astype(jnp.bfloat16)
    query_grad = (
        jnp.einsum("bhqk,bkhd->bqhd", score_grad, key_heads, preferred_element_type=jnp.float32)
        * scale_factor
    )
    key_grad = (
        jnp.einsum("bhqk,bqhd->bkhd", score_grad, queries, preferred_element_type=jnp.float32)
        * scale_factor
    )
    value_grad = jnp.einsum(
        "bhqk,bqhd->bkhd",
        probs_again.astype(jnp.bfloat16),
        attended_grad,
        preferred_element_type=jnp.float32,
    )
    mixed_grad = jnp.stack([query_grad, key_grad, value_grad], axis=2).astype(jnp.bfloat16)
    mixed_grad = mixed_grad.reshape(group_rows, 3 * heads_here * head_size)
    qkv_grad = lax.dot_general(
        mixed_grad, normed, (((0,), (0,)), ((), ())), preferred_element_type=jnp.float32
    )
    normed_grad = lax.psum_scatter(
        jnp.dot(mixed_grad, qkv_back, preferred_element_type=jnp.float32).astype(jnp.bfloat16),
        "tensor",
        scatter_dimension=0,
        tiled=True,
    ).astype(jnp.float32)
    _, first_pull = jax.vjp(layer_norm, block_in, norm_w[0], norm_w[1])
    input_part, gain_one, bias_one = first_pull(normed_grad)
    input_grad = residual_grad + input_part
    tile_grads = jnp.concatenate(
        [
            qkv_grad.reshape(3 * heads_here, head_size, model_width),
            out_proj_grad.reshape(heads_here, head_size, model_width),
            jnp.stack([in_expert_grad, out_expert_grad], axis=1).reshape(
                EXPERTS * 2 * tile_runs, head_size, model_width
            ),
            jnp.zeros((1, head_size, model_width), jnp.float32),
        ],
        axis=0,
    )
    tile_of_slot = (
        jnp.full((dp_count * slot_width,), tile_total, jnp.int32)
        .at[positions]
        .set(jnp.arange(tile_total, dtype=jnp.int32))
    )
    bank_grad = lax.psum_scatter(tile_grads[tile_of_slot], "dp", scatter_dimension=0, tiled=True)
    norm_grad, router_total = lax.psum(
        (jnp.stack([gain_one, bias_one, gain_two, bias_two]), router_grad), ("dp", "tensor")
    )
    bank_first, bank_second, bank_new = adamw_update(
        bank_w[0], bank_m[0], bank_v[0], bank_grad, rate_bank, weight_decay
    )
    norm_first, norm_second, norm_new = adamw_update(
        norm_w, norm_m, norm_v, norm_grad, rate_norm, 0.0
    )
    router_first, router_second, router_new = adamw_update(
        router_w, router_m, router_v, router_total, rate_router, weight_decay
    )
    return (
        block_out,
        input_grad,
        bank_first[None],
        bank_second[None],
        bank_new[None],
        norm_first,
        norm_second,
        norm_new,
        router_first,
        router_second,
        router_new,
    )


def solution(mesh):
    placed = (
        P(("dp", "tensor"), None),
        P(("dp", "tensor"), None),
        P("tensor", "dp", None, None),
        P("tensor", "dp", None, None),
        P("tensor", "dp", None, None),
        P(),
        P(),
        P(),
        P(),
        P(),
        P(),
        P("dp", None),
        P("dp", None),
        P(),
    )
    return jax.shard_map(
        on_device,
        mesh=mesh,
        in_specs=placed,
        out_specs=(
            P(("dp", "tensor"), None),
            P(("dp", "tensor"), None),
            P("tensor", "dp", None, None),
            P("tensor", "dp", None, None),
            P("tensor", "dp", None, None),
            P(),
            P(),
            P(),
            P(),
            P(),
            P(),
        ),
        check_vma=False,
    )
```

profile of v0, /device:TPU:1, one launch (start us, length us, event | category | flops | bytes accessed | tf_op | source)
XLA Modules:
  0.0 825.6 jit_solution(6208754026985711449)
XLA Ops:
  20.3 9.0 %scatter_custom_fusion = s32[1576]{0:T(1024)S(1)} fusion(s32[1576]{0:T(1024)S(1)} %fusion.51, s32[1576]{0:T(1024)S(1)} %iota.21, s32[]{:T(128)} %constant.47.clone.1), kind=kCustom, calls=%fused_computation.154 | custom fusion | bytes 6308 | tf_op jit(solution)/shard_map/scatter | solution.py:55
  29.8 8.8 %gather_fusion.1 = s32[1576]{0:T(1024)S(1)} fusion(s32[1576]{0:T(1024)S(1)} %reshape.284, s32[2048]{0:T(1024)S(1)} %pad_clamp_fusion.3), kind=kCustom, calls=%fused_computation.1 | custom fusion | bytes 18912 | tf_op jit(solution)/shard_map/gather | solution.py:56
  40.4 8.8 %gather_fusion.2 = s32[1576]{0:T(1024)S(1)} fusion(s32[1576]{0:T(1024)S(1)} %fusion.43, s32[2048]{0:T(1024)S(1)} %pad_clamp_fusion.2), kind=kCustom, calls=%fused_computation.2 | custom fusion | bytes 18912 | tf_op jit(solution)/shard_map/gather | solution.py:61
  51.3 110.0 %all-gather.11.cloned.1.call-done = bf16[1,224,64,768]{3,2,0,1:T(8,128)(2,1)} async-done(((bf16[1,28,64,768]{3,2,0,1:T(8,128)(2,1)}), bf16[1,224,64,768]{3,2,0,1:T(8,128)(2,1)}) %all-gather.11.cloned.1.call-update) | async-done | bytes 22020112 | tf_op jit(solution)/shard_map/all_gather | solution.py:113
  161.3 15.1 %gather_fusion = bf16[108,64,768]{2,1,0:T(8,128)(2,1)} fusion(bf16[224,64,768]{2,1,0:T(8,128)(2,1)} %bitcast.164, s32[1024]{0:T(1024)S(1)} %pad_clamp_fusion.5), kind=kCustom, calls=%fused_computation | custom fusion | bytes 21234096 | tf_op jit(solution)/shard_map/gather | solution.py:113
  195.4 27.4 %fusion = bf16[200,768]{1,0:T(8,128)(2,1)S(1)} fusion(bf16[788,768]{1,0:T(8,128)(2,1)S(1)} %convolution_convert_fusion), kind=kCustom, calls=%all-reduce-scatter | all-reduce-scatter fusion | flops 614401 | bytes 1518080
  231.3 8.8 %scatter_custom_fusion.1 = s32[1773]{0:T(1024)S(1)} fusion(s32[1576]{0:T(1024)S(1)} %fusion.52, s32[1576]{0:T(1024)S(1)} %add_select_fusion, s32[]{:T(128)} %constant.55.clone.1), kind=kCustom, calls=%fused_computation.156 | custom fusion | bytes 7096 | tf_op jit(solution)/shard_map/scatter | solution.py:65
  258.0 8.6 %slice.101 = bf16[96,64,768]{2,1,0:T(8,128)(2,1)} slice(bf16[108,64,768]{2,1,0:T(8,128)(2,1)} %gather_fusion), slice={[12:108], [0:64], [0:768]} | slice | bytes 18874368 | tf_op jit(solution)/shard_map/slice | solution.py:76
  269.9 19.7 %gather_fusion.8 = f32[1576]{0:T(1024)S(1)} fusion(f32[788,4]{0,1:T(4,128)S(1)} %fusion.46, s32[1576]{0:T(1024)S(1)} %reshape.364), kind=kCustom, calls=%fused_computation.8 | custom fusion | bytes 25216 | tf_op jit(solution)/shard_map/jit(take_along_axis)/gather | solution.py:153
  290.5 9.3 %scatter_custom_fusion.2 = f32[1773]{0:T(1024)S(1)} fusion(s32[1576]{0:T(1024)S(1)} %fusion.52, f32[1576]{0:T(1024)S(1)} %reshape.390, f32[]{:T(128)} %constant.43.clone.1), kind=kCustom, calls=%fused_computation.152 | custom fusion | bytes 7096 | tf_op jit(solution)/shard_map/scatter | solution.py:180
  352.2 10.0 %gather_fusion.4 = f32[1576,768]{1,0:T(8,128)} fusion(f32[1773,768]{1,0:T(8,128)} %concatenate.16, s32[2048]{0:T(1024)S(1)} %copy-done.2), kind=kCustom, calls=%fused_computation.4 | custom fusion | bytes 9689248 | tf_op jit(solution)/shard_map/gather | solution.py:165
  362.2 6.9 reshape.333
  374.4 10.2 %gather_fusion.6 = f32[1576,768]{1,0:T(8,128)} fusion(f32[1773,768]{1,0:T(8,128)} %concatenate.18, s32[2048]{0:T(1024)S(1)} %copy-done.2), kind=kCustom, calls=%fused_computation.6 | custom fusion | bytes 9689248 | tf_op jit(solution)/shard_map/gather | solution.py:203
  384.6 6.9 reshape.353
  391.5 9.5 %reduce_sum.217 = bf16[788,768]{1,0:T(8,128)(2,1)} reduce(f32[788,2,768]{2,1,0:T(2,128)} %reshape.353, f32[]{:T(128)} %constant.43.clone.1), dimensions={1}, to_apply=%region_19.20 | reduce | flops 605184 | bytes 6051844 | tf_op jit(solution)/shard_map/reduce_sum | solution.py:203
  401.1 13.3 %multiply_reduce_fusion = (bf16[788,2]{1,0:T(8,128)(2,1)}, bf16[788,768]{1,0:T(8,128)(2,1)}) fusion(f32[788,2,768]{2,1,0:T(2,128)} %reshape.333, f32[788,768]{1,0:T(8,128)S(1)} %copy-done.7, f32[788,2]{1,0:T(8,128)S(1)} %copy.119), kind=kLoop, calls=%fused_computation.32 | loop fusion | flops 4234712 | bytes 8482032 | tf_op jit(solution)/shard_map/reduce_sum | solution.py:176
  414.4 27.9 %fusion.78 = (bf16[200,768]{1,0:T(8,128)(2,1)S(1)}, bf16[208,2]{1,0:T(8,128)(2,1)S(1)}) fusion(bf16[788,768]{1,0:T(8,128)(2,1)} %reduce_sum.217, bf16[788,2]{1,0:T(8,128)(2,1)} %get-tuple-element.11), kind=kCustom, calls=%all-reduce-scatter.6 | all-reduce-scatter fusion | flops 616066 | bytes 1522064
  455.3 11.1 %convolution_bitcast_fusion = f32[4,1,768,768]{3,2,0,1:T(8,128)} fusion(f32[4,443,768]{2,1,0:T(8,128)} %reshape.299, f32[4,443]{1,0:T(4,128)S(1)} %mul.397, f32[4,443,768]{2,1,0:T(8,128)} %copy-done.63), kind=kOutput, calls=%fused_computation.40 | convolution fusion | flops 2105306112 | bytes 20331440 | tf_op jit(solution)/shard_map/ecf,ecd->efd/dot_general | solution.py:190
  503.9 14.6 %maximum_maximum_fusion = f32[109,64,768]{2,1,0:T(8,128)} fusion(f32[96,64,768]{2,1,0:T(8,128)} %bitcast.155, f32[3,64,768]{2,1,0:T(8,128)S(1)} %fusion.87, f32[9,64,768]{2,1,0:T(8,128)S(1)} %fusion.86, f32[109]{0:T(128)S(1)} %copy-done.59), kind=kLoop, calls=%fused_computation.13 | loop fusion | flops 16072704 | bytes 42664372 | tf_op jit(solution)/shard_map/concatenate | solution.py:278
  518.5 29.5 %gather_fusion.7 = f32[224,64,768]{2,1,0:T(8,128)} fusion(f32[109,64,768]{2,1,0:T(8,128)} %maximum_maximum_fusion, s32[1024]{0:T(1024)} %pad_clamp_fusion.4), kind=kCustom, calls=%fused_computation.7 | custom fusion | bytes 88081280 | tf_op jit(solution)/shard_map/gather | solution.py:294
  552.7 44.8 %fusion.77 = (bf16[200,768]{1,0:T(8,128)(2,1)S(1)}, bf16[200,768]{1,0:T(8,128)(2,1)S(1)}) fusion(bf16[788,768]{1,0:T(8,128)(2,1)} %get-tuple-element.12, bf16[788,768]{1,0:T(8,128)(2,1)} %convolution_convert_fusion.1), kind=kCustom, calls=%all-reduce-scatter.5 | all-reduce-scatter fusion | flops 1228801 | bytes 3035648
  608.8 42.4 %all-reduce.15 = (f32[4,768]{1,0:T(4,128)S(1)}, f32[768,4]{0,1:T(4,128)S(1)}) all-reduce(f32[4,768]{1,0:T(4,128)S(1)} %pad_maximum_fusion.1, f32[768,4]{0,1:T(4,128)S(1)} %fusion.61), channel_id=1, replica_groups=mesh['dp'=8,'tensor'=4] {'dp','tensor'}, use_global_device_ids=true, to_apply=%region_39.40 | all-reduce | flops 6144 | bytes 49152 | tf_op jit(solution)/shard_map/psum | solution.py:295
  657.0 146.3 %reduce-scatter.12.cloned.1.call-done = f32[28,64,768]{2,1,0:T(8,128)} async-done(((f32[224,64,768]{2,1,0:T(8,128)}), f32[28,64,768]{2,1,0:T(8,128)}) %reduce-scatter.12.cloned.1.call-update) | async-done | bytes 5505040 | tf_op jit(solution)/shard_map/reduce_scatter | solution.py:294
  803.3 14.9 %fusion.13 = (f32[1,28,64,768]{3,2,1,0:T(8,128)}, f32[1,28,64,768]{3,2,1,0:T(8,128)}, f32[1,28,64,768]{3,2,1,0:T(8,128)}) fusion(f32[1,28,64,768]{3,2,1,0:T(8,128)} %param.16, f32[28,64,768]{2,1,0:T(8,128)} %reduce-scatter.12.cloned.1.call-done, f32[1,28,64,768]{3,2,1,0:T(8,128)} %param.17, f32[1,28,64,768]{3,2,1,0:T(8,128)} %param.18), kind=kLoop, calls=%fused_computation.27 | loop fusion | flops 17891328 | bytes 38535168 | tf_op jit(solution)/shard_map/broadcast_in_dim | solution.py:312
  (323 shorter events, 194.6 us)
Async XLA Ops:
  7.2 42.5 %all-gather.13.cloned.1.call-start = ((), (), s32[]{:S(2)}) async-start(), calls=%async_computation.3 | async-start | bytes 1536000 | tf_op jit(solution)/shard_map/all_gather | solution.py:122
  11.2 255.3 %copy-start.36 = (f32[768]{0:T(1024)}, f32[768]{0:T(1024)S(1)}, u32[]{:S(2)}) copy-start(f32[768]{0:T(1024)S(1)} %get-tuple-element.19) | copy-start | bytes 9220
  13.8 147.5 %all-gather.11.cloned.1.call-start = ((), (), s32[]{:S(2)}) async-start(), calls=%async_computation.2 | async-start | bytes 24772608 | tf_op jit(solution)/shard_map/all_gather | solution.py:113
  18.5 223.6 %all-gather.17.cloned.1.call-start = ((), (), s32[]{:S(2)}) async-start(), calls=%async_computation.5 | async-start | bytes 1536000 | tf_op jit(solution)/shard_map/all_gather | solution.py:174
  19.3 248.3 %all-gather.15.cloned.1.call-start = ((), (), s32[]{:S(2)}) async-start(), calls=%async_computation.4 | async-start | bytes 1536000 | tf_op jit(solution)/shard_map/all_gather | solution.py:149
  222.8 2.6 collective-permute-start
  227.3 257.0 %all-gather.19.cloned.1.call-start = ((), (), s32[]{:S(2)}) async-start(), calls=%async_computation.6 | async-start | bytes 1536000 | tf_op jit(solution)/shard_map/all_gather | solution.py:229
  401.0 46.1 %copy-start.6 = (f32[197,768]{1,0:T(8,128)S(1)}, f32[197,768]{1,0:T(8,128)}, u32[]{:S(2)}) copy-start(f32[197,768]{1,0:T(8,128)} %copy-done.5) | copy-start | bytes 1815556
  401.0 46.1 %copy-start.32 = (f32[768,4]{0,1:T(4,128)S(1)}, f32[768,4]{0,1:T(4,128)}, u32[]{:S(2)}) copy-start(f32[768,4]{0,1:T(4,128)} %param.22) | copy-start | bytes 36868
  401.1 46.9 %copy-start.55 = (f32[197]{0:T(256)S(1)}, f32[197]{0:T(256)}, u32[]{:S(2)}) copy-start(f32[197]{0:T(256)} %copy-done.54) | copy-start | bytes 2368
  442.3 3.4 collective-permute-start.3
  443.6 3.0 collective-permute-start.2
  450.0 353.3 %reduce-scatter.12.cloned.1.call-start = ((), (), s32[]{:S(2)}) async-start(), calls=%async_computation.1 | async-start | bytes 49545216 | tf_op jit(solution)/shard_map/reduce_scatter | solution.py:294
  549.2 51.4 %copy-start.23 = (bf16[197,768]{1,0:T(8,128)(2,1)S(1)}, bf16[197,768]{1,0:T(8,128)(2,1)}, u32[]{:S(2)}) copy-start(bf16[197,768]{1,0:T(8,128)(2,1)} %copy-done.22) | copy-start | bytes 907780
  549.2 56.0 %copy-start.4 = (f32[197,768]{1,0:T(8,128)S(1)}, f32[197,768]{1,0:T(8,128)}, u32[]{:S(2)}) copy-start(f32[197,768]{1,0:T(8,128)} %param.14) | copy-start | bytes 1815556
  549.2 56.0 %copy-start.35 = (f32[768]{0:T(1024)S(1)}, f32[768]{0:T(1024)}, u32[]{:S(2)}) copy-start(f32[768]{0:T(1024)} %copy-done.34) | copy-start | bytes 9220
  549.2 56.0 %copy-start.42 = (f32[197]{0:T(256)S(1)}, f32[197]{0:T(256)}, u32[]{:S(2)}) copy-start(f32[197]{0:T(256)} %copy-done.41) | copy-start | bytes 2368
  549.2 56.3 %copy-start.53 = (f32[197]{0:T(256)S(1)}, f32[197]{0:T(256)}, u32[]{:S(2)}) copy-start(f32[197]{0:T(256)} %copy-done.52) | copy-start | bytes 2368
  549.3 56.3 %copy-start.50 = (f32[197]{0:T(256)S(1)}, f32[197]{0:T(256)}, u32[]{:S(2)}) copy-start(f32[197]{0:T(256)} %copy-done.49) | copy-start | bytes 2368
  552.7 98.5 %copy-start.40 = (f32[4,768]{1,0:T(4,128)S(1)}, f32[4,768]{1,0:T(4,128)}, u32[]{:S(2)}) copy-start(f32[4,768]{1,0:T(4,128)} %param.19) | copy-start | bytes 36868
  552.7 103.2 %copy-start.9 = (f32[197,768]{1,0:T(8,128)S(1)}, f32[197,768]{1,0:T(8,128)}, u32[]{:S(2)}) copy-start(f32[197,768]{1,0:T(8,128)} %copy-done.8) | copy-start | bytes 1815556
  552.7 103.2 %copy-start.12 = (f32[197,768]{1,0:T(8,128)S(1)}, f32[197,768]{1,0:T(8,128)}, u32[]{:S(2)}) copy-start(f32[197,768]{1,0:T(8,128)} %param.15) | copy-start | bytes 1815556
  597.5 5.3 collective-permute-start.4
  600.9 5.1 collective-permute-start.1
  (56 other events, 832.0 us)
Sparse Core Ops, SparseCore 0:
  13.9 32.7 all-gather.12
  49.2 112.1 all-gather.10
  163.5 30.2 all-gather.16
  227.4 31.0 all-gather.14
  450.1 34.1 all-gather.18
  548.2 255.0 reduce-scatter.11
where the time goes:
time: 833 us; the launch traced here: 826 us
  waiting for transfers between devices  262 us (31%)
  local copies, waits for them, and re-layouts  254 us (30%)
  blocking collectives  142 us (17%)
  other arithmetic  83.3 us (10%)
  matrix products  55.8 us (7%)
  between operations  17.4 us (2%)
  starting transfers between devices  10.1 us (1%)
    reduce_scatter x1, waiting for transfers between devices, on_device(): lax.psum_scatter(tile_grads[tile_of_slot], 'dp', scatter_dimension=0, til...  146 us
    all_gather x1, waiting for transfers between devices, on_device(): weight_tiles = lax.all_gather(bank_low, 'dp', axis=0, tiled=True)[positions]  110 us
    unnamed x3, blocking collectives  100 us
    psum x1, blocking collectives, on_device(): lax.psum((jnp.stack([gain_one, bias_one, gain_two, bias_two]), router_gra...  42.4 us
    unnamed x162, local copies, waits for them, and re-layouts  29.6 us
    gather x1, local copies, waits for them, and re-layouts, on_device(): tile_grads[tile_of_slot]  29.5 us
    gather x5, local copies, waits for them, and re-layouts, on_device(): gate_pair = jnp.take_along_axis(router_probs, expert_ids, axis=1)  20.6 us
    gather x2, local copies, waits for them, and re-layouts, on_device(): second_part = jnp.sum(dispatch_pad[pair_slot], axis=1)  17.1 us
  transfers between devices with their start and end apart: 11, of which 4 were waited for; matrix products, arithmetic and copies ran while one was open for 28% of the time, Pallas kernels for 0%

commit v1 on v0

v1 whole, which is shorter than its diff:
```python
import functools

import jax
import jax.numpy as jnp
from jax import lax
from jax.experimental import pallas as pl
from jax.experimental.pallas import tpu as pltpu
from jax.sharding import PartitionSpec as P

HEADS = 12
FF = 3072
SEQ = 197
EXPERTS = 4
STEP = 10
CAPACITY = 443

ROWS = -(-SEQ // 16) * 16
SLOTS = -(-CAPACITY // 16) * 16
ROUTER_ROWS = 16
VMEM_BYTES = 56 * 1024 * 1024

norm_epsilon = 1e-06
beta_first = 0.9
beta_second = 0.95
adam_epsilon = 1e-08
weight_decay = 0.1
rate_bank = 0.06
rate_norm = 0.25
rate_router = 0.05
highest = lax.Precision.HIGHEST
low_type = jnp.bfloat16
full_type = jnp.float32


def dot_nn(left, right):
    return lax.dot_general(left, right, (((1,), (0,)), ((), ())), preferred_element_type=full_type)


def dot_nt(left, right):
    return lax.dot_general(left, right, (((1,), (1,)), ((), ())), preferred_element_type=full_type)


def dot_tn(left, right):
    return lax.dot_general(left, right, (((0,), (0,)), ((), ())), preferred_element_type=full_type)


def adamw_update(weights, first_old, second_old, grad_total, step_rate, decay_rate):
    first_new = beta_first * first_old + (1.0 - beta_first) * grad_total
    second_new = beta_second * second_old + (1.0 - beta_second) * grad_total * grad_total
    first_scale = step_rate / (1.0 - beta_first**STEP)
    second_scale = 1.0 / (1.0 - beta_second**STEP)
    weights_new = weights * (1.0 - step_rate * decay_rate) - first_new * first_scale / (
        jnp.sqrt(second_new * second_scale) + adam_epsilon
    )
    return (first_new, second_new, weights_new)


def call(body, grid, in_specs, out_specs, out_shape, scratch=(), prefetch=0, flops=0, moved=0):
    return pl.pallas_call(
        body,
        grid_spec=pltpu.PrefetchScalarGridSpec(
            num_scalar_prefetch=prefetch,
            grid=grid,
            in_specs=in_specs,
            out_specs=out_specs,
            scratch_shapes=list(scratch),
        ),
        out_shape=out_shape,
        compiler_params=pltpu.CompilerParams(vmem_limit_bytes=VMEM_BYTES),
        cost_estimate=pl.CostEstimate(flops=flops, bytes_accessed=moved, transcendentals=0),
    )


def whole(shape):
    return pl.BlockSpec(shape, lambda *_: (0,) * len(shape))


def shaped(shape, kind):
    return jax.ShapeDtypeStruct(shape, kind)


def row_mask(rows):
    return lax.broadcasted_iota(jnp.int32, (rows, 1), 0) < SEQ


def normalize(values):
    center = values - jnp.mean(values, axis=-1, keepdims=True)
    variance = jnp.mean(center * center, axis=-1, keepdims=True)
    spread = lax.rsqrt(variance + norm_epsilon)
    return center * spread, spread


def norm_back(scaled, spread, grad_rows, gain_row):
    inner = grad_rows * gain_row
    mean_one = jnp.mean(inner, axis=-1, keepdims=True)
    mean_two = jnp.mean(inner * scaled, axis=-1, keepdims=True)
    return spread * (inner - mean_one - scaled * mean_two)


def first_kernel(block_ref, grad_ref, out_ref):
    mask = row_mask(ROWS)
    model = block_ref.shape[1]
    scaled, _ = normalize(jnp.where(mask, block_ref[...], 0.0))
    out_ref[:, :model] = jnp.where(mask, scaled, 0.0).astype(low_type)
    out_ref[:, model:] = jnp.where(mask, grad_ref[...], 0.0).astype(low_type)


def dispatch_kernel(pair_count, col_ref, row_ref, pick_ref, place_ref, slot_row, slot_col):
    expert = pl.program_id(0)
    tokens = row_ref.shape[1]
    chunk = ROWS // 2

    @pl.when(expert == 0)
    def _():
        row_zero = row_ref[0:1, :]
        row_one = row_ref[1:2, :]

        def ones(condition):
            return jnp.where(condition, 1.0, 0.0)

        bounds = [float(e * pair_count) for e in range(1, EXPERTS)]
        below = [
            jnp.sum(ones(row_zero < b) + ones(row_one < b), axis=1, keepdims=True) for b in bounds
        ]

        def slots(keys, lower):
            base = jnp.zeros_like(keys)
            index = jnp.zeros_like(keys)
            for bound, count in zip(bounds, below):
                base = jnp.where(keys >= bound, jnp.broadcast_to(count, keys.shape), base)
                index = index + ones(keys >= bound)
            placed = lower - base
            kept = jnp.logical_and(placed < CAPACITY, keys < float(EXPERTS * pair_count))
            return jnp.where(kept, index * SLOTS + placed, -1.0)

        def step(i, carried):
            low_zero, low_one = carried
            start = pl.multiple_of(i * chunk, 8)
            keys = col_ref[pl.ds(start, chunk), :]
            zero = keys[:, 0:1]
            one = keys[:, 1:2]
            before_zero = jnp.sum(
                ones(row_zero < zero) + ones(row_one < zero), axis=1, keepdims=True
            )
            before_one = jnp.sum(ones(row_zero < one) + ones(row_one < one), axis=1, keepdims=True)
            slot_col[pl.ds(start, chunk), 0:1] = slots(zero, before_zero)
            slot_col[pl.ds(start, chunk), 1:2] = slots(one, before_one)
            low_zero = low_zero + jnp.sum(
                ones(zero < row_zero) + ones(one < row_zero), axis=0, keepdims=True
            )
            low_one = low_one + jnp.sum(
                ones(zero < row_one) + ones(one < row_one), axis=0, keepdims=True
            )
            return low_zero, low_one

        nothing = jnp.zeros((1, tokens), full_type)
        low_zero, low_one = lax.fori_loop(0, tokens // chunk, step, (nothing, nothing))
        slot_row[0:1, :] = slots(row_zero, low_zero)
        slot_row[1:2, :] = slots(row_one, low_one)

    begin = expert * SLOTS
    down = (lax.broadcasted_iota(jnp.int32, (SLOTS, 1), 0) + begin).astype(full_type)
    hit = jnp.logical_or(slot_row[0:1, :] == down, slot_row[1:2, :] == down)
    pick_ref[0] = jnp.where(hit, 1.0, 0.0).astype(low_type)

    @pl.when(expert == 0)
    def _():
        across = lax.broadcasted_iota(jnp.int32, (1, EXPERTS * SLOTS), 1).astype(full_type)
        hit = jnp.logical_or(slot_col[:, 0:1] == across, slot_col[:, 1:2] == across)
        place_ref[...] = jnp.where(hit, 1.0, 0.0).astype(low_type)


def fetch_tiles(table_ref, pieces, first, last, start, offset=0):
    for piece in pieces:

        def step(j, carried, piece=piece, offset=offset):
            tile = table_ref[offset + j]

            @pl.when(jnp.logical_and(tile >= first, tile < last))
            def _():
                start(piece.at[j], tile)

            return carried

        lax.fori_loop(0, piece.shape[0], step, 0)
        offset += piece.shape[0]


def softmax_rows(scores):
    valid = lax.broadcasted_iota(jnp.int32, scores.shape, 1) < SEQ
    scores = jnp.where(valid, scores, -1e30)
    top = jnp.max(scores, axis=-1, keepdims=True)
    powers = jnp.exp(scores - top)
    return powers / jnp.sum(powers, axis=-1, keepdims=True)


def attend_kernel(heads, banks, table_ref, *refs):
    bank, refs = refs[:banks], refs[banks:]
    scaled_ref, norm_ref = refs[:2]
    normed_ref, mixed_ref, attended_ref, branch_ref, tiles, semaphore = refs[-6:]
    count, head, model = tiles.shape

    @pl.when(pl.program_id(0) == 0)
    def _():
        def start(source, tile):
            pltpu.make_async_copy(source, tiles.at[tile], semaphore).start()

        fetch_tiles(table_ref, bank, 0, count, start)
        pltpu.make_async_copy(tiles, tiles, semaphore).wait()

    width = heads * head
    proj_in = tiles[: 3 * heads].reshape(3 * width, model)
    proj_out = tiles[3 * heads :].reshape(width, model)
    mask = row_mask(ROWS)
    rows = scaled_ref[...].astype(full_type) * norm_ref[0:1, :] + norm_ref[1:2, :]
    rows = jnp.where(mask, rows, 0.0).astype(low_type)
    normed_ref[...] = rows
    mixed = dot_nt(rows, proj_in).astype(low_type)
    mixed_ref[0] = mixed
    parts = []
    for h in range(heads):
        query, key, value = (
            mixed[:, p * width + h * head : p * width + (h + 1) * head] for p in range(3)
        )
        probs = softmax_rows(dot_nt(query, key) * head**-0.5).astype(low_type)
        parts.append(dot_nn(probs, value))
    attended = jnp.where(mask, jnp.concatenate(parts, axis=1), 0.0).astype(low_type)
    attended_ref[0] = attended
    branch_ref[...] = dot_nn(attended, proj_out).astype(low_type)


def second_kernel(block_ref, norm_ref, branch_ref, residual_ref, second_ref):
    mask = row_mask(ROWS)
    residual = jnp.where(mask, block_ref[...], 0.0) + branch_ref[...].astype(full_type)
    residual_ref[...] = residual
    scaled, _ = normalize(residual)
    rows = scaled * norm_ref[2:3, :] + norm_ref[3:4, :]
    second_ref[...] = jnp.where(mask, rows, 0.0).astype(low_type)


def gelu_pair(values):
    factor = 0.7978845608028654
    square = values * values
    bent = jnp.tanh(factor * values * (1.0 + 0.044715 * square))
    half = 0.5 * (1.0 + bent)
    slope = half + 0.5 * factor * values * (1.0 - bent * bent) * (1.0 + 0.134145 * square)
    return values * half, slope


def expert_probs(router_rows, second_rows):
    logits = dot_nt(router_rows, second_rows)
    real = lax.broadcasted_iota(jnp.int32, logits.shape, 0) < EXPERTS
    logits = jnp.where(real, logits, -1e30)
    powers = jnp.exp(logits - jnp.max(logits, axis=0, keepdims=True))
    return powers / jnp.sum(powers, axis=0, keepdims=True)


def pick_kernel(cotangent_ref, pick_ref, _, rows_ref):
    rows_ref[0] = dot_nn(pick_ref[0], cotangent_ref[...]).astype(low_type)


def prepare_kernel(base, banks, table_ref, *refs):
    bank, refs = refs[:banks], refs[banks:]
    tiles_ref, semaphore = refs[-2:]
    count = tiles_ref.shape[0]

    def start(source, tile):
        pltpu.make_async_copy(source, tiles_ref.at[tile - base], semaphore).start()

    fetch_tiles(table_ref, bank, base, base + count, start)
    pltpu.make_async_copy(tiles_ref, tiles_ref, semaphore).wait()


def expert_kernel(images, runs, place_of_ref, *refs):
    tiles_ref, grads_ref, second_ref, router_ref, pick_ref, place_ref = refs[:6]
    first_ref, sent_ref, kept_ref, gated_ref, piece_ref = refs[6:11]
    probs, pair_grad, rows_back, place, stage, out_semaphore, place_semaphore = refs[11:]
    expert = pl.program_id(0)
    model = second_ref.shape[1]
    hidden_width = runs * tiles_ref.shape[2]
    place_copy = pltpu.make_async_copy(place_ref, place, place_semaphore)

    @pl.when(expert == 0)
    def _():
        place_copy.start()
        probs[...] = expert_probs(router_ref[...], second_ref[...])
        pair_grad[...] = jnp.zeros_like(pair_grad)

    weight_in = tiles_ref[0, :runs].reshape(hidden_width, model)
    weight_out = tiles_ref[0, runs:].reshape(hidden_width, model)
    pick = pick_ref[0]
    pick_full = pick.astype(full_type)
    gate = jnp.sum(pick_full * probs[pl.ds(expert, 1), :], axis=1, keepdims=True)
    grad_rows = grads_ref[0].astype(full_type)
    back = (gate * grad_rows).astype(low_type)
    rows = dot_nn(pick, second_ref[...]).astype(low_type)
    hidden = dot_nt(rows, weight_in)
    act_grad = dot_nt(back, weight_out)
    activated, slope = gelu_pair(hidden)
    activated = activated.astype(low_type)
    hidden_grad = (act_grad * slope).astype(low_type)
    returned = dot_nn(activated, weight_out)
    here = pl.ds(pl.multiple_of(expert * SLOTS, SLOTS), SLOTS)
    rows_back[here, :] = dot_nn(hidden_grad, weight_in).astype(low_type)
    gate_grad = jnp.sum(grad_rows * returned, axis=1, keepdims=True)
    pair_grad[pl.ds(expert, 1), :] = jnp.sum(pick_full * gate_grad, axis=0, keepdims=True)
    gated_ref[0] = (gate * returned).astype(low_type)
    slot = lax.rem(expert, 2)
    sent_count = 1 + sent_ref.shape[0]

    def settle(which, m):
        copy = stage.at[which, m]
        pltpu.make_async_copy(copy, copy, out_semaphore.at[which, m]).wait()

    for m, (left, right) in enumerate(((hidden_grad, rows), (activated, back))):

        @pl.when(expert >= 2)
        def _(m=m):
            settle(slot, m)

        stage[slot, m] = dot_tn(left, right).astype(low_type).reshape(stage.shape[2:])
        target = place_of_ref[2 * expert + m]
        copy = (stage.at[slot, m], out_semaphore.at[slot, m])

        @pl.when(target == 0)
        def _(copy=copy):
            pltpu.make_async_copy(copy[0], first_ref, copy[1]).start()

        @pl.when(jnp.logical_and(target > 0, target < sent_count))
        def _(target=target, copy=copy):
            pltpu.make_async_copy(copy[0], sent_ref.at[target - 1], copy[1]).start()

        @pl.when(target >= sent_count)
        def _(target=target, copy=copy):
            pltpu.make_async_copy(copy[0], kept_ref.at[target - sent_count], copy[1]).start()

    @pl.when(expert == EXPERTS - 1)
    def _():
        place_copy.wait()
        total = dot_nn(place[...], rows_back[...])
        for s in range(images):
            first = s * (ROWS + ROUTER_ROWS)
            last = first + ROWS + ROUTER_ROWS
            middle = first + ROWS
            here = slice(s * ROWS, (s + 1) * ROWS)
            piece_ref[first:middle, :] = total[here, :].astype(low_type)
            piece_ref[middle:last, :] = jnp.zeros((ROUTER_ROWS, model), low_type)
            piece_ref[middle:last, :ROWS] = pair_grad[:, here].astype(low_type)
        for which in range(2):
            for m in range(2):
                settle(which, m)


def combine_kernel(gated_ref, place_ref, out_ref):
    out_ref[...] = dot_nn(place_ref[...], gated_ref[...]).astype(low_type)


def second_back_kernel(
    residual_ref, grad_ref, second_ref, router_ref, norm_ref, piece_ref, *refs
):
    rows_ref, low_ref, small_ref = refs[-3:]
    mask = row_mask(ROWS)
    total = piece_ref[...].astype(full_type)
    second = second_ref[...]
    router_rows = router_ref[...]
    probs = expert_probs(router_rows, second)
    probs_grad = total[ROWS:, :ROWS]
    logit_grad = probs * (probs_grad - jnp.sum(probs * probs_grad, axis=0, keepdims=True))
    second_grad = total[:ROWS, :] + lax.dot_general(
        logit_grad,
        router_rows.astype(full_type),
        (((0,), (0,)), ((), ())),
        precision=highest,
        preferred_element_type=full_type,
    )
    router_grad = lax.dot_general(
        logit_grad,
        second.astype(full_type),
        (((1,), (0,)), ((), ())),
        precision=highest,
        preferred_element_type=full_type,
    )
    second_grad = jnp.where(mask, second_grad, 0.0)
    scaled, spread = normalize(residual_ref[...])
    part = norm_back(scaled, spread, second_grad, norm_ref[2:3, :])
    rows = jnp.where(mask, grad_ref[...] + part, 0.0)
    rows_ref[...] = rows
    low_ref[...] = rows.astype(low_type)
    small_ref[0:1, :] = jnp.sum(second_grad * scaled, axis=0, keepdims=True)
    small_ref[1:2, :] = jnp.sum(second_grad, axis=0, keepdims=True)
    small_ref[2 : 2 + EXPERTS, :] = router_grad[:EXPERTS, :]
    small_ref[2 + EXPERTS :, :] = jnp.zeros((6 - EXPERTS, small_ref.shape[1]), full_type)


def attend_back_kernel(images, heads, banks, table_ref, core_ref, *refs):
    bank, refs = refs[:banks], refs[banks:]
    (
        branch_ref,
        scaled_ref,
        normed_ref,
        mixed_ref,
        attended_ref,
        small_two_ref,
        own_ref,
        other_ref,
        piece_ref,
        small_ref,
        tiles,
        cotangent,
        normed,
        mixed_grad,
        attended,
        semaphore,
    ) = refs
    count, head, model = tiles.shape
    image = pl.program_id(0)

    @pl.when(image == 0)
    def _():
        def start(source, tile):
            pltpu.make_async_copy(source, tiles.at[tile], semaphore).start()

        fetch_tiles(table_ref, bank, 0, count, start)
        pltpu.make_async_copy(tiles, tiles, semaphore).wait()
        small_ref[0:2, :] = jnp.zeros((2, model), full_type)
        small_ref[2:, :] = small_two_ref[:6, :]

    width = heads * head
    scale = head**-0.5
    proj_in = tiles[: 3 * heads].reshape(3 * width, model)
    proj_out = tiles[3 * heads :].reshape(width, model)
    here = pl.ds(pl.multiple_of(image * ROWS, ROWS), ROWS)
    branch = branch_ref[...]
    cotangent[here, :] = branch
    normed[here, :] = normed_ref[...]
    attended[here, :] = attended_ref[0]
    attended_grad = dot_nt(branch, proj_out).astype(low_type)
    mixed = mixed_ref[0]
    parts = [[], [], []]
    for h in range(heads):
        query, key, value = (
            mixed[:, p * width + h * head : p * width + (h + 1) * head] for p in range(3)
        )
        above = attended_grad[:, h * head : (h + 1) * head]
        probs = softmax_rows(dot_nt(query, key) * scale)
        weight_grad = dot_nt(above, value)
        inner = jnp.sum(probs * weight_grad, axis=-1, keepdims=True)
        score_grad = (probs * (weight_grad - inner)).astype(low_type)
        parts[0].append(dot_nn(score_grad, key) * scale)
        parts[1].append(dot_tn(score_grad, query) * scale)
        parts[2].append(dot_tn(probs.astype(low_type), above))
    grads = jnp.concatenate(parts[0] + parts[1] + parts[2], axis=1).astype(low_type)
    mixed_grad[here, :] = grads
    back = dot_nn(grads, proj_in)
    piece_ref[...] = back.astype(low_type)
    small_ref[0:1, :] += jnp.sum(back * scaled_ref[...].astype(full_type), axis=0, keepdims=True)
    small_ref[1:2, :] += jnp.sum(back, axis=0, keepdims=True)

    @pl.when(image == images - 1)
    def _():
        tile_grads = jnp.concatenate(
            [
                dot_tn(mixed_grad[...], normed[...]).astype(low_type),
                dot_tn(attended[...], cotangent[...]).astype(low_type),
            ],
            axis=0,
        )
        rows = count // 2 * head
        rest = tile_grads.reshape(2, rows, model)

        @pl.when(core_ref[0] == 0)
        def _():
            own_ref[:rows, :] = rest[0]
            other_ref[:rows, :] = rest[1]

        @pl.when(core_ref[0] == 1)
        def _():
            own_ref[:rows, :] = rest[1]
            other_ref[:rows, :] = rest[0]

        for ref in (own_ref, other_ref):
            ref[rows:, :] = split_sums(small_ref[...])


def split_sums(rows):
    high = rows.astype(low_type)
    low = (rows - high.astype(full_type)).astype(low_type)
    return jnp.concatenate([high.astype(full_type), low.astype(full_type)], axis=0).astype(low_type)


def join_sums(rows):
    wide = rows.astype(full_type)
    return wide[:8, :] + wide[8:, :]


def near_add_kernel(count, left_ref, right_ref, *refs):
    outs = refs[-count:]
    rows = left_ref.shape[0] - 16
    total = left_ref[:rows, :].astype(full_type) + right_ref[:rows, :].astype(full_type)
    sums = split_sums(join_sums(left_ref[rows:, :]) + join_sums(right_ref[rows:, :]))
    outs[0][:rows, :] = total.astype(low_type)
    outs[-1][outs[-1].shape[0] - 16 :, :] = sums


def last_sum_kernel(images, here_ref, *refs):
    pieces, out_ref, held = refs[:images], refs[-2], refs[-1]
    for s in range(images):
        held[lax.rem(here_ref[0] + s, images)] = join_sums(pieces[s][...])
    total = held[0]
    for s in range(1, images):
        total = total + held[s]
    out_ref[...] = total


def first_back_kernel(block_ref, grad_ref, norm_ref, residual_ref, piece_ref, added_ref, *refs):
    grad_out, block_out = refs[-2:]
    mask = row_mask(ROWS)
    total = jnp.where(mask, piece_ref[...].astype(full_type), 0.0)
    scaled, spread = normalize(jnp.where(mask, block_ref[...], 0.0))
    grad_out[...] = grad_ref[...] + norm_back(scaled, spread, total, norm_ref[0:1, :])
    block_out[...] = residual_ref[...] + added_ref[...].astype(full_type)


def bank_kernel(pieces, plan_ref, *refs):
    olds = refs[:3]
    sources = refs[3 : 3 + pieces]
    outs = refs[-9:-6]
    held, fresh, grads, held_semaphore, fresh_semaphore, grad_semaphore = refs[-6:]
    ahead, behind, width = held.shape[0], fresh.shape[0], grads.shape[0]
    count = plan_ref[2 * width]

    def load(j):
        slot, row = plan_ref[j], lax.rem(j, ahead)
        for k in range(3):
            pltpu.make_async_copy(
                olds[k].at[0, slot], held.at[row, k], held_semaphore.at[row, k]
            ).start()

    def settle(ref, semaphore):
        pltpu.make_async_copy(ref, ref, semaphore).wait()

    for j in range(ahead - 1):
        pl.when(j < count)(functools.partial(load, j))

    def start(source, slot):
        pltpu.make_async_copy(source, grads.at[slot], grad_semaphore.at[slot]).start()

    fetch_tiles(plan_ref, sources, 0, width, start, 2 * width + 1)

    def step(j, carried):
        pl.when(j + ahead - 1 < count)(lambda: load(j + ahead - 1))
        slot, row, out_row = plan_ref[j], lax.rem(j, ahead), lax.rem(j, behind)
        used = plan_ref[width + slot]
        for k in range(3):
            settle(held.at[row, k], held_semaphore.at[row, k])
        pl.when(used == 1)(lambda: settle(grads.at[slot], grad_semaphore.at[slot]))
        grad = jnp.where(used == 1, grads[slot].astype(full_type), 0.0)
        updated = adamw_update(*(held[row, k] for k in range(3)), grad, rate_bank, weight_decay)
        for k, value in enumerate(updated):
            pl.when(j >= behind)(
                lambda k=k: settle(fresh.at[out_row, k], fresh_semaphore.at[out_row, k])
            )
            fresh[out_row, k] = value
            pltpu.make_async_copy(
                fresh.at[out_row, k], outs[k].at[0, slot], fresh_semaphore.at[out_row, k]
            ).start()
        return carried

    lax.fori_loop(0, count, step, 0)
    for row in range(behind):
        for k in range(3):
            pl.when(row < count)(
                lambda row=row, k=k: settle(fresh.at[row, k], fresh_semaphore.at[row, k])
            )


def after_kernel(*refs):
    del refs


def pack_kernel(slot_ref, core_ref, weight_ref, *refs):
    outs = refs[-2:]
    half = outs[0].shape[0]
    for t in range(half):
        for which in range(2):
            slot = slot_ref[lax.rem(core_ref[0] + which, 2) * half + t]
            tile = weight_ref[0, jnp.maximum(slot, 0)]
            outs[which][t] = jnp.where(slot >= 0, tile, 0.0).astype(low_type)


def round_kernel(weight_ref, *refs):
    refs[-1][...] = weight_ref[0].astype(low_type)


def gather_rows(rows):
    return lax.all_gather(rows, "tensor", axis=0, tiled=True)


def scatter_rows(rows):
    return lax.psum_scatter(rows, "tensor", scatter_dimension=0, tiled=True)


def collect_rows(rows):
    size = lax.axis_size("tensor")
    return [
        lax.ppermute(rows, "tensor", [((i + s) % size, i) for i in range(size)])
        for s in range(1, size)
    ]


def butterfly(values, axis):
    size = lax.axis_size(axis)
    bit = 1
    while bit < size:
        values = values + lax.ppermute(values, axis, [(i, i ^ bit) for i in range(size)])
        bit *= 2
    return values


CORE, ALONG_X, ALONG_Y = 1, 2, 4


def swap(values):
    size = lax.axis_size("dp")
    return lax.ppermute(values, "dp", [(i, i ^ CORE) for i in range(size)])


def hop(values, second=False):
    size = lax.axis_size("dp")
    along = (ALONG_Y, ALONG_X) if second else (ALONG_X, ALONG_Y)
    return lax.ppermute(values, "dp", [(i, i ^ along[i & CORE]) for i in range(size)])


any_spec = pl.BlockSpec(memory_space=pl.ANY)


def after(values, before):
    if not before:
        return values
    return pl.pallas_call(
        after_kernel,
        in_specs=[any_spec] * (1 + len(before)),
        out_specs=any_spec,
        out_shape=shaped(values.shape, values.dtype),
        input_output_aliases={0: 0},
    )(values, *before)


def region(flag, body, *operands):
    shapes = jax.eval_shape(body, *operands)

    def skipped(*_):
        return jax.tree.map(lambda a: jnp.zeros(a.shape, a.dtype), shapes)

    return lax.cond(flag, body, skipped, *operands)


def add_low(*parts):
    total = parts[0].astype(full_type)
    for part in parts[1:]:
        total = total + part.astype(full_type)
    return total.astype(low_type)


def total_tiles(grads):
    count = lax.axis_size("dp")
    pad = -grads.shape[0] % count
    if pad:
        grads = jnp.pad(grads, ((0, pad), (0, 0), (0, 0)))
    owned = lax.psum_scatter(grads, "dp", scatter_dimension=0, tiled=True)
    return lax.all_gather(owned, "dp", axis=0, tiled=True)


def on_device(
    block_in,
    out_grad,
    bank_w,
    bank_m,
    bank_v,
    norm_w,
    norm_m,
    norm_v,
    router_w,
    router_m,
    router_v,
    expert_ids,
    fill_rank,
    owner_list,
):
    dp_count = lax.axis_size("dp")
    images = lax.axis_size("tensor")
    row_count, model = block_in.shape
    group_rows = expert_ids.shape[0]
    slot_width = bank_w.shape[1]
    head = bank_w.shape[2]
    heads = HEADS // images
    runs = FF // (images * head)
    tile_total = owner_list.shape[0]
    near_tiles = 4 * heads
    far_tiles = tile_total - near_tiles
    pair_count = 2 * group_rows
    tokens = images * ROWS
    assert row_count == SEQ and group_rows == images * SEQ

    me = lax.axis_index("dp")
    paired = dp_count == 8
    core = jnp.bitwise_and(me, CORE if paired else 0).astype(jnp.int32)
    flag = owner_list[0] >= 0
    number = jnp.arange(tile_total, dtype=jnp.int32)
    same = owner_list[:, None] == owner_list[None, :]
    slot = jnp.sum(
        jnp.where(jnp.logical_and(same, number[None, :] < number[:, None]), 1, 0), axis=1
    ).astype(jnp.int32)
    near_slots = min(near_tiles, slot_width)
    far_slots = slot_width - near_slots
    owners = jnp.arange(dp_count, dtype=jnp.int32)
    if paired:
        owners = jnp.bitwise_xor(owners, me)
    tile_at = jnp.logical_and(
        owner_list[None, None, :] == owners[:, None, None],
        slot[None, None, :] == jnp.arange(slot_width, dtype=jnp.int32)[None, :, None],
    )
    tile_at = jnp.sum(jnp.where(tile_at, number[None, None, :] + 1, 0), axis=2) - 1
    tile_at = tile_at.astype(jnp.int32)
    slot_here = jnp.where(owner_list == me, slot, -1)
    slot_here = slot_here.astype(jnp.int32)
    slot_number = jnp.arange(slot_width, dtype=jnp.int32)
    slot_used = jnp.sum(
        jnp.where(slot_here[None, :] == slot_number[:, None], 1, 0), axis=1
    ).astype(jnp.int32)

    full_rows = pl.BlockSpec((ROWS, model), lambda *_: (0, 0))
    small = whole((4, model))
    low_rows = shaped((ROWS, model), low_type)
    wide_rows = shaped((ROWS, model), full_type)

    scaled_rows = call(
        first_kernel,
        (1,),
        [full_rows, full_rows],
        whole((ROWS, 2 * model)),
        shaped((ROWS, 2 * model), low_type),
    )(block_in, out_grad)
    both = gather_rows(scaled_rows)
    scaled_half = pl.BlockSpec((ROWS, model), lambda s, *_: (s, 0))
    grads_half = pl.BlockSpec((tokens, model), lambda *_: (0, 1))
    image_rows = pl.BlockSpec((ROWS, model), lambda s, *_: (s, 0))

    group = slot_width // 2 if slot_width % 2 == 0 else 1
    slab = call(
        round_kernel,
        (slot_width // group,),
        [pl.BlockSpec((1, group, head, model), lambda j: (0, j, 0, 0)), any_spec],
        pl.BlockSpec((group, head, model), lambda j: (j, 0, 0)),
        shaped((slot_width, head, model), low_type),
    )(bank_w, scaled_rows)

    keys = (expert_ids * pair_count + fill_rank).astype(full_type).reshape(images, SEQ, 2)
    keys = jnp.pad(
        keys, ((0, 0), (0, ROWS - SEQ), (0, 0)), constant_values=float(2 * EXPERTS * pair_count)
    ).reshape(tokens, 2)
    router_rows = jnp.pad(router_w.astype(low_type).T, ((0, ROUTER_ROWS - EXPERTS), (0, 0)))

    half = near_tiles // 2
    half_shape = (half, head, model)

    def dispatch(keys):
        return call(
            functools.partial(dispatch_kernel, pair_count),
            (EXPERTS,),
            [whole((tokens, 2)), whole((2, tokens))],
            [
                pl.BlockSpec((1, SLOTS, tokens), lambda e: (e, 0, 0)),
                whole((tokens, EXPERTS * SLOTS)),
            ],
            [
                shaped((EXPERTS, SLOTS, tokens), low_type),
                shaped((tokens, EXPERTS * SLOTS), low_type),
            ],
            scratch=[pltpu.VMEM((2, tokens), full_type), pltpu.VMEM((tokens, 2), full_type)],
        )(keys, keys.T)

    if paired:
        near, beside = call(
            pack_kernel,
            (1,),
            [pl.BlockSpec((1, near_slots, head, model), lambda j, *_: (0, 0, 0, 0)), any_spec],
            [whole(half_shape)] * 2,
            [shaped(half_shape, low_type)] * 2,
            prefetch=2,
        )(slot_here[:near_tiles], core.reshape(1), bank_w, slab)
        pick, place = dispatch(keys)
        near = add_low(near, swap(beside))
        near = add_low(near, hop(near))
        slab_beside = after(swap(slab), [near])
        first = hop(slab)
        first_beside = hop(slab_beside)
        near = after(add_low(near, hop(near, second=True)), [both, pick])
        near_banks = [near, swap(near)]
        near_table = jnp.concatenate(
            [jnp.arange(half, dtype=jnp.int32) + lax.rem(core + i, 2) * half for i in range(2)]
        )
    else:
        pick, place = dispatch(keys)
        near_banks = [lax.all_gather(slab, "dp", axis=0, tiled=True)]
        near_table = tile_at.reshape(-1)

    width = heads * head
    all_rows = whole((tokens, model))
    all_shape = shaped((tokens, model), low_type)
    mixed_shape = (images, ROWS, 3 * width)
    attended_shape = (images, ROWS, width)
    mixed_spec = pl.BlockSpec((1,) + mixed_shape[1:], lambda s, *_: (s, 0, 0))
    attended_spec = pl.BlockSpec((1,) + attended_shape[1:], lambda s, *_: (s, 0, 0))
    normed, mixed, attended, branch = call(
        functools.partial(attend_kernel, heads, len(near_banks)),
        (images,),
        [any_spec] * len(near_banks) + [scaled_half, small, any_spec],
        [image_rows, mixed_spec, attended_spec, image_rows],
        [all_shape, shaped(mixed_shape, low_type), shaped(attended_shape, low_type), all_shape],
        scratch=[pltpu.VMEM((near_tiles, head, model), low_type), pltpu.SemaphoreType.DMA(())],
        prefetch=1,
    )(near_table, *near_banks, both, norm_w, slab)
    residual, second_rows = call(
        second_kernel,
        (1,),
        [full_rows, small, full_rows],
        [full_rows, full_rows],
        [wide_rows, low_rows],
    )(block_in, norm_w, scatter_rows(branch))
    picked_grads = call(
        pick_kernel,
        (EXPERTS,),
        [grads_half, pl.BlockSpec((1, SLOTS, tokens), lambda e: (e, 0, 0)), any_spec],
        pl.BlockSpec((1, SLOTS, model), lambda e: (e, 0, 0)),
        shaped((EXPERTS, SLOTS, model), low_type),
    )(both, pick, second_rows)
    second = gather_rows(second_rows)
    mine = jnp.where(core == 0, ALONG_X, ALONG_Y)
    other = ALONG_X + ALONG_Y - mine
    far_away = ALONG_X + ALONG_Y
    if paired:
        first = after(first, [first_beside])
        across = after(hop(first, second=True), [picked_grads])
        far_pieces = [
            (0, 0, slab),
            (CORE, 0, slab_beside),
            (mine, 0, first),
            (mine + CORE, 0, first_beside),
            (far_away, 0, across),
            (other + CORE, 0, swap(first)),
            (other, 0, swap(first_beside)),
        ]
        cuts = 4 if slot_width % 4 == 0 else 1
        size = slot_width // cuts
        far_pieces += [
            (far_away + CORE, i, swap(across[i : i + size])) for i in range(0, slot_width, size)
        ]
        far_banks = [p for _, _, p in far_pieces]
        far_table = jnp.concatenate(
            [
                lax.dynamic_index_in_dim(tile_at, r, 0, keepdims=False)[f : f + p.shape[0]]
                for r, f, p in far_pieces
            ]
        )
    else:
        far_banks, far_table = near_banks, near_table

    near_here = slot_here[:near_tiles]

    def plan(wanted, table):
        place = jnp.cumsum(wanted) - 1
        listed = jnp.logical_and(wanted[None, :] == 1, place[None, :] == slot_number[:, None])
        slots = jnp.sum(jnp.where(listed, slot_number[None, :], 0), axis=1).astype(jnp.int32)
        count = jnp.sum(wanted).astype(jnp.int32).reshape(1)
        return jnp.concatenate([slots, slot_used, count, table])

    if paired:

        def far_tables(*order):
            return jnp.concatenate(
                [
                    lax.dynamic_slice_in_dim(
                        slot_here, near_tiles + jnp.bitwise_xor(me, r) * runs, runs, 0
                    )
                    for r in order
                ]
            )

        def held(table):
            return jnp.sum(
                jnp.where(table[None, :] == slot_number[:, None], 1, 0), axis=1
            ).astype(jnp.int32)

        tables = [
            far_tables(0, CORE, mine, other + CORE),
            far_tables(mine + CORE, other, far_away, far_away + CORE),
            jnp.concatenate(
                [
                    lax.dynamic_slice_in_dim(near_here, lax.rem(core + i, 2) * half, half, 0)
                    for i in range(2)
                ]
            ),
        ]
        wanted = [held(table) for table in tables]
        tables.append(jnp.zeros((0,), jnp.int32))
        wanted.append(1 - slot_used)
        plans = [after(plan(w, t), [second_rows]) for w, t in zip(wanted, tables)]
    else:
        plans = []

    def update(table, sources, olds):
        ahead, behind = 4, 3
        return pl.pallas_call(
            functools.partial(bank_kernel, len(sources)),
            grid_spec=pltpu.PrefetchScalarGridSpec(
                num_scalar_prefetch=1,
                grid=(1,),
                in_specs=[any_spec] * (3 + len(sources) + len(olds)),
                out_specs=[any_spec] * 3,
                scratch_shapes=[
                    pltpu.VMEM((ahead, 3, head, model), full_type),
                    pltpu.VMEM((behind, 3, head, model), full_type),
                    pltpu.VMEM((slot_width, head, model), low_type),
                    pltpu.SemaphoreType.DMA((ahead, 3)),
                    pltpu.SemaphoreType.DMA((behind, 3)),
                    pltpu.SemaphoreType.DMA((slot_width,)),
                ],
            ),
            out_shape=[shaped(bank_w.shape, full_type)] * 3,
            input_output_aliases={4 + len(sources) + i: i for i in range(len(olds))},
            compiler_params=pltpu.CompilerParams(vmem_limit_bytes=VMEM_BYTES),
        )(table, bank_w, bank_m, bank_v, *sources, *olds)

    blocks = 2 * EXPERTS
    tiles_shape = (runs, head, model)
    half_blocks = (EXPERTS,) + tiles_shape
    block_number = jnp.arange(blocks, dtype=jnp.int32)
    if paired:
        order = [far_away + CORE, other, other + CORE, CORE, far_away, mine + CORE, mine, 0]
        order = jnp.bitwise_xor(me, jnp.stack([jnp.asarray(r, me.dtype) for r in order]))
        place_of = jnp.sum(
            jnp.where(order[None, :] == block_number[:, None], block_number[None, :], 0), axis=1
        )
    else:
        place_of = block_number
    expert_rows = pl.BlockSpec((1, SLOTS, model), lambda e, *_: (e, 0, 0))
    piece_shape = (ROWS + ROUTER_ROWS, model)
    pieces_shape = (images * piece_shape[0], model)
    expert_tiles = (EXPERTS, 2 * runs, head, model)

    tiles = call(
        functools.partial(prepare_kernel, near_tiles, len(far_banks)),
        (1,),
        [any_spec] * (len(far_banks) + 1 + len(plans)),
        whole((far_tiles, head, model)),
        shaped((far_tiles, head, model), low_type),
        scratch=[pltpu.SemaphoreType.DMA(())],
        prefetch=1,
    )(far_table, *far_banks, second_rows, *plans)
    sent_first, sent, kept, gated, pieces = call(
        functools.partial(expert_kernel, images, runs),
        (EXPERTS,),
        [
            pl.BlockSpec((1,) + expert_tiles[1:], lambda e, *_: (e, 0, 0, 0)),
            expert_rows,
            all_rows,
            whole((ROUTER_ROWS, model)),
            pl.BlockSpec((1, SLOTS, tokens), lambda e, *_: (e, 0, 0)),
            any_spec,
        ],
        [any_spec, any_spec, any_spec, expert_rows, whole(pieces_shape)],
        [
            shaped(tiles_shape, low_type),
            shaped((EXPERTS - 1,) + tiles_shape, low_type),
            shaped(half_blocks, low_type),
        ]
        + [shaped((EXPERTS, SLOTS, model), low_type), shaped(pieces_shape, low_type)],
        scratch=[
            pltpu.VMEM((ROUTER_ROWS, tokens), full_type),
            pltpu.VMEM((ROUTER_ROWS, tokens), full_type),
            pltpu.VMEM((EXPERTS * SLOTS, model), low_type),
            pltpu.VMEM((tokens, EXPERTS * SLOTS), low_type),
            pltpu.VMEM((2, 2) + tiles_shape, low_type),
            pltpu.SemaphoreType.DMA((2, 2)),
            pltpu.SemaphoreType.DMA(()),
        ],
        prefetch=1,
    )(
        place_of.astype(jnp.int32),
        tiles.reshape(expert_tiles),
        picked_grads,
        second,
        router_rows,
        pick,
        place,
    )
    piece = scatter_rows(pieces)

    def combine(gated):
        return call(
            combine_kernel,
            (images,),
            [
                whole((EXPERTS * SLOTS, model)),
                pl.BlockSpec((ROWS, EXPERTS * SLOTS), lambda s: (s, 0)),
            ],
            image_rows,
            all_shape,
        )(gated.reshape(EXPERTS * SLOTS, model), place)

    def sum_far(sent_first, sent, kept, gated):
        across = add_low(kept[0], swap(sent_first))
        part = swap(after(sent, [across]))
        across = hop(across, second=True)
        combined = combine(gated)
        beside = hop(add_low(kept[1], part[0]))
        return combined, part, beside, add_low(kept[2], part[1], across)

    if paired:
        combined, part, beside, along = region(flag, sum_far, sent_first, sent, kept, gated)
        ordered = [along]
    else:
        combined, ordered = combine(gated), []

    residual_grad, branch_rows, small_two = call(
        second_back_kernel,
        (1,),
        [full_rows, full_rows, full_rows, whole((ROUTER_ROWS, model)), small, whole(piece_shape)]
        + [any_spec] * len(ordered),
        [full_rows, full_rows, whole((8, model))],
        [wide_rows, low_rows, shaped((8, model), full_type)],
    )(residual, out_grad, second_rows, router_rows, norm_w, piece, *ordered)
    branch_grads = gather_rows(branch_rows)

    if paired:

        def sum_own(kept, part, beside, along, plan):
            own = add_low(kept[3], part[2], hop(along), swap(beside))
            return update(plan, [], []), own, swap(own), hop(own)

        own_blocks = region(
            flag, sum_own, kept, part, beside, after(along, [branch_rows]), plans[3]
        )
    else:
        products = jnp.concatenate([sent_first[None], sent, kept], axis=0)
        products = products.reshape(far_tiles, head, model)
        far_sources = [total_tiles(products)]
        far_slots_here = [
            jnp.pad(
                slot_here[near_tiles:],
                (0, far_sources[0].shape[0] - far_tiles),
                constant_values=-1,
            )
        ]

    here = lax.axis_index("tensor").astype(jnp.int32).reshape(1)
    near_rows = half * head
    near_shape = (near_rows + 16, model)
    def add_near(left, right, before=(), apart=False):
        shapes = [(near_rows, model), (16, model)] if apart else [near_shape]
        out = call(
            functools.partial(near_add_kernel, len(shapes)),
            (1,),
            [whole(near_shape)] * 2 + [any_spec] * len(before),
            [whole(shape) for shape in shapes],
            [shaped(shape, low_type) for shape in shapes],
        )(left, right, *before)
        return out if apart else out[0]

    def attend_back(branch_grads, small_two):
        return call(
            functools.partial(attend_back_kernel, images, heads, len(near_banks)),
            (images,),
            [any_spec] * len(near_banks)
            + [image_rows, scaled_half, image_rows, mixed_spec, attended_spec]
            + [whole((8, model))],
            [whole(near_shape)] * 2 + [image_rows, whole((8, model))],
            [shaped(near_shape, low_type)] * 2 + [all_shape, shaped((8, model), full_type)],
            scratch=[
                pltpu.VMEM((near_tiles, head, model), low_type),
                pltpu.VMEM((tokens, model), low_type),
                pltpu.VMEM((tokens, model), low_type),
                pltpu.VMEM((tokens, 3 * width), low_type),
                pltpu.VMEM((tokens, width), low_type),
                pltpu.SemaphoreType.DMA(()),
            ],
            prefetch=2,
        )(
            near_table,
            core.reshape(1),
            *near_banks,
            branch_grads,
            both,
            normed,
            mixed,
            attended,
            small_two,
        )

    def third(branch_grads, small_two, plan, banks, own, own_beside, first):
        far = [hop(own_beside), hop(first, second=True)]
        early = [own, own_beside, first, swap(first)]
        near, beside, pieces, _ = attend_back(branch_grads, small_two)
        near = add_near(near, swap(beside))
        return near, pieces, far, update(plan, early, banks)

    combined = scatter_rows(combined)
    if paired:
        near, pieces, far, banks = region(
            flag, third, branch_grads, small_two, plans[0], *own_blocks
        )
        pieces = after(pieces, [combined])
    else:
        near_own, near_beside, pieces, sums = attend_back(branch_grads, small_two)
    pieces = scatter_rows(pieces)

    def finish(far, own, banks, plans):
        late = [p for block in far for p in (block, swap(block))]
        banks = update(plans[0], late, banks)
        own, sums = add_near(own, hop(own), banks[:1], apart=True)
        sums = [sums] + collect_rows(sums)
        sums = call(
            functools.partial(last_sum_kernel, images),
            (1,),
            [whole((16, model))] * images,
            whole((8, model)),
            shaped((8, model), full_type),
            scratch=[pltpu.VMEM((images, 8, model), full_type)],
            prefetch=1,
        )(here, *sums)
        own = add_low(own, after(hop(own, second=True), [sums]))
        tiles_here = own.reshape(half_shape)
        other_sums = hop(sums, second=True)
        banks = update(plans[1], [tiles_here, swap(tiles_here)], banks)
        sums = sums + after(other_sums, [banks[2]])
        return *banks, sums

    if paired:
        bank_first, bank_second, bank_new, sums = region(
            flag, finish, far, near, banks, plans[1:3]
        )
    else:
        near_grads = jnp.concatenate([near_own[:near_rows], near_beside[:near_rows]], axis=0)
        near_sources = [total_tiles(near_grads.reshape(near_tiles, head, model))]
        near_slots_here = [
            jnp.pad(near_here, (0, near_sources[0].shape[0] - near_tiles), constant_values=-1)
        ]
        sums = butterfly(butterfly(sums, "tensor"), "dp")
        table = jnp.concatenate([far_slots_here[0], near_slots_here[0]])
        bank_first, bank_second, bank_new = update(
            plan(jnp.ones((slot_width,), jnp.int32), table), far_sources + near_sources, []
        )
    input_grad, block_out = call(
        first_back_kernel,
        (1,),
        [full_rows, full_rows, small, full_rows, full_rows, full_rows, any_spec],
        [full_rows, full_rows],
        [shaped((SEQ, model), full_type)] * 2,
    )(block_in, residual_grad, norm_w, residual, pieces, combined, bank_new)
    norm_grad = sums[:4]
    router_total = sums[4:].T
    norm_first, norm_second, norm_new = adamw_update(
        norm_w, norm_m, norm_v, norm_grad, rate_norm, 0.0
    )
    router_first, router_second, router_new = adamw_update(
        router_w, router_m, router_v, router_total, rate_router, weight_decay
    )
    return (
        block_out,
        input_grad,
        bank_first,
        bank_second,
        bank_new,
        norm_first,
        norm_second,
        norm_new,
        router_first,
        router_second,
        router_new,
    )


def solution(mesh):
    rows = P(("dp", "tensor"), None)
    bank = P("tensor", "dp", None, None)
    return jax.shard_map(
        on_device,
        mesh=mesh,
        in_specs=(rows, rows, bank, bank, bank) + (P(),) * 6 + (P("dp", None), P("dp", None), P()),
        out_specs=(rows, rows, bank, bank, bank) + (P(),) * 6,
        check_vma=False,
    )
```

time: 833 us -> 342 us (0.41)
  local copies, waits for them, and re-layouts: 254 us -> 15 us
  waiting for transfers between devices: 262 us -> 103 us
  blocking collectives: 142 us -> 0 us
  Pallas kernels: 0 us -> 138 us
  other arithmetic: 83.3 us -> 24.4 us
  matrix products: 55.8 us -> 0 us
  starting transfers between devices: 10.1 us -> 44.4 us
    pallas_call x0 -> x33, Pallas kernels: none -> 138 us  [the longest x1 31.6 us: on_device(): call(functools.partial(expert_kernel, images, runs), (EXPERTS,), [pl.Bloc...]
    reduce_scatter x1 -> x4, waiting for transfers between devices: 146 us -> 10.7 us  [scatter_rows(): return lax.psum_scatter(rows, 'tensor', scatter_dimension=0, tiled=True)]
    gather x17 -> x0, local copies, waits for them, and re-layouts: 130 us -> none  [the longest x1 29.5 us: on_device(): tile_grads[tile_of_slot]]
    unnamed x3 -> x0, blocking collectives: 100 us -> none
    all_gather x5 -> x3, waiting for transfers between devices: 116 us -> 18.3 us  [gather_rows(): return lax.all_gather(rows, 'tensor', axis=0, tiled=True)]
    ppermute x0 -> x35, waiting for transfers between devices: none -> 73.7 us  [the longest x14 58.4 us: hop(): lax.ppermute(values, 'dp', [(i, i ^ along[i & CORE]) for i in range(size)])]
    dot_general x22 -> x0, matrix products: 55.8 us -> none  [the longest x1 11.1 us: on_device(): jnp.einsum('ecf,ecd->efd', activated, returned_grad, preferred_element_ty...]
    ppermute x0 -> x35, starting transfers between devices: none -> 43.9 us  [the longest x14 23.5 us: hop(): lax.ppermute(values, 'dp', [(i, i ^ along[i & CORE]) for i in range(size)])]
  transfers between devices with their start and end apart: 11 -> 42, of which waited for: 4 -> 19; matrix products, arithmetic and copies ran while one was open for 28% -> 10% of each run, Pallas kernels for 0% -> 27%
where the time goes in v1:
time: 342 us; the launch traced here: 340 us
  Pallas kernels  138 us (40%)
  waiting for transfers between devices  103 us (30%)
  starting transfers between devices  44.4 us (13%)
  other arithmetic  24.4 us (7%)
  local copies, waits for them, and re-layouts  15 us (4%)
  between operations  14.6 us (4%)
    ppermute x14, waiting for transfers between devices, hop(): lax.ppermute(values, 'dp', [(i, i ^ along[i & CORE]) for i in range(size)])  58.4 us
    pallas_call x1, Pallas kernels, on_device(): call(functools.partial(expert_kernel, images, runs), (EXPERTS,), [pl.Bloc...  31.6 us
    pallas_call x4, Pallas kernels, update(): pl.pallas_call(functools.partial(bank_kernel, len(sources)), grid_spec=pl...  25.6 us
    ppermute x14, starting transfers between devices, hop(): lax.ppermute(values, 'dp', [(i, i ^ along[i & CORE]) for i in range(size)])  23.5 us
    all_gather x3, waiting for transfers between devices, gather_rows(): return lax.all_gather(rows, 'tensor', axis=0, tiled=True)  18.3 us
    convert_element_type x8, other arithmetic, add_low(): return total.astype(low_type)  16.2 us
    pallas_call x1, Pallas kernels, attend_back(): call(functools.partial(attend_back_kernel, images, heads, len(near_banks)...  15.9 us
    ppermute x18, starting transfers between devices, swap(): return lax.ppermute(values, 'dp', [(i, i ^ CORE) for i in range(size)])  15.4 us
  transfers between devices with their start and end apart: 42, of which 19 were waited for; matrix products, arithmetic and copies ran while one was open for 10% of the time, Pallas kernels for 27%

profile of v1, /device:TPU:1, one launch (start us, length us, event | category | flops | bytes accessed | tf_op | source)
XLA Modules:
  0.0 340.1 jit_solution(5233602139744868568)
XLA Ops:
  24.3 7.6 %collective-permute-done.22 = bf16[6,64,768]{2,1,0:T(8,128)(2,1)S(1)} collective-permute-done((bf16[6,64,768]{2,1,0:T(8,128)(2,1)S(1)}, bf16[6,64,768]{2,1,0:T(8,128)(2,1)S(1)}, u32[]{:S(2)}, u32[]{:S(2)}) %collective-permute-start.22) | collective-permute-done | bytes 589856 | tf_op jit(solution)/shard_map/ppermute | solution.py:631
  36.8 9.2 %shard_map.224 = (bf16[4,448,832]{2,1,0:T(8,128)(2,1)}, bf16[832,1792]{1,0:T(8,128)(2,1)}) custom-call(f32[832,2]{1,0:T(8,128)} %copy.62.col_ref, f32[2,832]{1,0:T(2,128)} %bitcast.54), custom_call_target="tpu_custom_call" | custom-call | tf_op jit(solution)/shard_map/pallas_call | solution.py:768
  51.3 18.2 %all-gather.4.cloned.1.call-done.refs_1_.refs_2_.cotangent_ref = bf16[832,1536]{1,0:T(8,128)(2,1)} async-done(((bf16[208,1536]{1,0:T(8,128)(2,1)}), bf16[832,1536]{1,0:T(8,128)(2,1)}) %all-gather.4.cloned.1.call-update) | async-done | bytes 2555920 | tf_op jit(solution)/shard_map/all_gather | solution.py:596
  72.1 10.9 %shard_map.226 = (bf16[832,768]{1,0:T(8,128)(2,1)}, bf16[4,208,576]{2,1,0:T(8,128)(2,1)}, bf16[4,208,192]{2,1,0:T(8,128)(2,1)}, bf16[832,768]{1,0:T(8,128)(2,1)}) custom-call(s32[12]{0:T(128)S(1)} %pad_add_fusion.table_ref, bf16[6,64,768]{2,1,0:T(8,128)(2,1)S(1)} %shard_map.225.refs_0_, bf16[6,64,768]{2,1,0:T(8,128)(2,1)} %collective-permute-done.24.refs_1_, ...), custom_call_target="tpu_custom_call" | custom-call | tf_op jit(solution)/shard_map/pallas_call | solution.py:815
  84.1 13.1 %collective-permute-done.27.refs_1_.refs_3_ = bf16[28,64,768]{2,1,0:T(8,128)(2,1)} collective-permute-done((bf16[28,64,768]{2,1,0:T(8,128)(2,1)}, bf16[28,64,768]{2,1,0:T(8,128)(2,1)}, u32[]{:S(2)}, u32[]{:S(2)}) %collective-permute-start.27) | collective-permute-done | bytes 2752544 | tf_op jit(solution)/shard_map/ppermute | solution.py:631
  101.5 10.7 %reduce-scatter.5.cloned.1.call-done.branch_ref = bf16[208,768]{1,0:T(8,128)(2,1)} async-done(((bf16[832,768]{1,0:T(8,128)(2,1)}), bf16[208,768]{1,0:T(8,128)(2,1)}) %reduce-scatter.5.cloned.1.call-update) | async-done | bytes 319504 | tf_op jit(solution)/shard_map/reduce_scatter | solution.py:600
  115.8 6.1 %shard_map.230.refs_1_ = bf16[4,448,768]{2,1,0:T(8,128)(2,1)} custom-call(bf16[832,1536]{1,0:T(8,128)(2,1)S(1)} %copy-done.3, bf16[4,448,832]{2,1,0:T(8,128)(2,1)} %get-tuple-element.207.refs_2_.pick_ref.refs_4_, bf16[208,768]{1,0:T(8,128)(2,1)} %get-tuple-element.210._.refs_1_.refs_11_.second_ref), custom_call_target="tpu_custom_call" | custom-call | tf_op jit(solution)/shard_map/pallas_call | solution.py:831
  122.0 7.8 %collective-permute-done.28.refs_0_ = bf16[28,64,768]{2,1,0:T(8,128)(2,1)} collective-permute-done((bf16[28,64,768]{2,1,0:T(8,128)(2,1)}, bf16[28,64,768]{2,1,0:T(8,128)(2,1)}, u32[]{:S(2)}, u32[]{:S(2)}) %collective-permute-start.28) | collective-permute-done | bytes 2752544 | tf_op jit(solution)/shard_map/ppermute | solution.py:631
  140.3 8.3 %shard_map.236 = bf16[96,64,768]{2,1,0:T(8,128)(2,1)} custom-call(s32[224]{0:T(256)} %concatenate.35.table_ref, bf16[28,64,768]{2,1,0:T(8,128)(2,1)} %shard_map.222.refs_0_.refs_4_, bf16[28,64,768]{2,1,0:T(8,128)(2,1)} %shard_map.228.refs_1_, bf16[28,64,768]{2,1,0:T(8,128)(2,1)} %shard_map.229.refs_2_, ...), custom_call_target="tpu_custom_call" | custom-call | tf_op jit(solution)/shard_map/pallas_call | solution.py:952
  148.6 31.6 %shard_map.237 = (bf16[12,64,768]{2,1,0:T(8,128)(2,1)}, bf16[3,12,64,768]{3,2,1,0:T(8,128)(2,1)}, bf16[4,12,64,768]{3,2,1,0:T(8,128)(2,1)}, bf16[4,448,768]{2,1,0:T(8,128)(2,1)}, bf16[896,768]{1,0:T(8,128)(2,1)}) custom-call(s32[8]{0:T(128)} %select_reduce_fusion.13.place_of_ref, bf16[4,24,64,768]{3,2,1,0:T(8,128)(2,1)} %bitcast.50, ...), custom_call_target="tpu_custom_call" | custom-call | tf_op jit(solution)/shard_map/pallas_call | solution.py:961
  180.3 34.9 %conditional.4 = (bf16[832,768]{1,0:T(8,128)(2,1)}, bf16[3,12,64,768]{3,2,1,0:T(8,128)(2,1)}, bf16[12,64,768]{2,1,0:T(8,128)(2,1)}, bf16[12,64,768]{2,1,0:T(8,128)(2,1)}) conditional(s32[]{:T(128)} %bitcast.25, () %tuple.40, (bf16[4,448,768]{2,1,0:T(8,128)(2,1)}, bf16[832,1792]{1,0:T(8,128)(2,1)}, bf16[4,12,64,768]{3,2,1,0:T(8,128)(2,1)}, ...), branch_computations={%region_21.22_spmd, %region_22.23_spmd} | conditional | flops 8257536 | bytes 52035804 | solution.py:655
  188.3 4.5 %collective-permute-done.5 = bf16[3,12,64,768]{3,2,1,0:T(8,128)(2,1)} collective-permute-done((bf16[3,12,64,768]{3,2,1,0:T(8,128)(2,1)}, bf16[3,12,64,768]{3,2,1,0:T(8,128)(2,1)}, u32[]{:S(2)}, u32[]{:S(2)}) %collective-permute-start.5) | collective-permute-done | bytes 3538976 | tf_op jit(solution)/shard_map/cond/branch_1_fun/ppermute | solution.py:625
  196.5 5.6 %branch_1_fun.12 = bf16[832,768]{1,0:T(8,128)(2,1)} custom-call(bf16[1792,768]{1,0:T(8,128)(2,1)} %bitcast.51, bf16[832,1792]{1,0:T(8,128)(2,1)S(1)} %copy-done.4), custom_call_target="tpu_custom_call" | custom-call | tf_op jit(solution)/shard_map/cond/branch_1_fun/pallas_call | solution.py:1001
  202.1 4.3 %collective-permute-done.7 = bf16[12,64,768]{2,1,0:T(8,128)(2,1)S(1)} collective-permute-done((bf16[12,64,768]{2,1,0:T(8,128)(2,1)}, bf16[12,64,768]{2,1,0:T(8,128)(2,1)S(1)}, u32[]{:S(2)}, u32[]{:S(2)}) %collective-permute-start.7) | collective-permute-done | bytes 1179680 | tf_op jit(solution)/shard_map/cond/branch_1_fun/ppermute | solution.py:631
  209.6 5.6 %collective-permute-done.6 = bf16[12,64,768]{2,1,0:T(8,128)(2,1)} collective-permute-done((bf16[12,64,768]{2,1,0:T(8,128)(2,1)S(1)}, bf16[12,64,768]{2,1,0:T(8,128)(2,1)}, u32[]{:S(2)}, u32[]{:S(2)}) %collective-permute-start.6) | collective-permute-done | bytes 1179680 | tf_op jit(solution)/shard_map/cond/branch_1_fun/ppermute | solution.py:631
  219.6 35.2 %conditional.5 = (f32[1,28,64,768]{3,2,1,0:T(8,128)}, f32[1,28,64,768]{3,2,1,0:T(8,128)}, f32[1,28,64,768]{3,2,1,0:T(8,128)}, bf16[12,64,768]{2,1,0:T(8,128)(2,1...) conditional(s32[]{:T(128)} %bitcast.25, () %tuple.43, (s32[57]{0:T(128)S(1)}, ...), branch_computations={%region_23.24_spmd, %region_24.25_spmd} | conditional | flops 4718592 | bytes 46792940 | solution.py:655
  221.8 13.8 %collective-permute-done.8 = bf16[12,64,768]{2,1,0:T(8,128)(2,1)S(1)} collective-permute-done((bf16[12,64,768]{2,1,0:T(8,128)(2,1)}, bf16[12,64,768]{2,1,0:T(8,128)(2,1)S(1)}, u32[]{:S(2)}, u32[]{:S(2)}) %collective-permute-start.8) | collective-permute-done | bytes 1179680 | tf_op jit(solution)/shard_map/cond/branch_1_fun/ppermute | solution.py:631
  241.8 12.3 %branch_1_fun.14 = (f32[1,28,64,768]{3,2,1,0:T(8,128)}, f32[1,28,64,768]{3,2,1,0:T(8,128)}, f32[1,28,64,768]{3,2,1,0:T(8,128)}) custom-call(s32[57]{0:T(128)S(1)} %get-tuple-element.96.plan_ref, f32[1,28,64,768]{3,2,1,0:T(8,128)S(1)} %copy-done, f32[1,28,64,768]{3,2,1,0:T(8,128)} %get-tuple-element.98.refs_1_, f32[1,28,64,768]{3,2,1,0:T(8,128)} %get-tuple-element.99.refs_2_), custom_call_target="tpu_custom_call" | custom-call | tf_op jit(solution)/shard_map/cond/branch_1_fun/pallas_call | solution.py:914
  254.9 31.4 %conditional.6 = (bf16[400,768]{1,0:T(8,128)(2,1)}, bf16[832,768]{1,0:T(8,128)(2,1)}, bf16[12,64,768]{2,1,0:T(8,128)(2,1)}, bf16[12,64,768]{2,1,0:T(8,128)(2,1)}...) conditional(s32[]{:T(128)} %bitcast.25, () %tuple.42, (s32[]{:T(128)}, ...), branch_computations={%region_25.26_spmd, %region_26.27_spmd} | conditional | bytes 41091344 | solution.py:655
  259.3 15.9 %branch_1_fun.15 = (bf16[400,768]{1,0:T(8,128)(2,1)}, bf16[400,768]{1,0:T(8,128)(2,1)}, bf16[832,768]{1,0:T(8,128)(2,1)}, f32[8,768]{1,0:T(8,128)}) custom-call(s32[12]{0:T(128)S(1)} %get-tuple-element.107.table_ref, s32[1]{0:T(128)} %bitcast.6.core_ref, bf16[6,64,768]{2,1,0:T(8,128)(2,1)} %get-tuple-element.109.refs_0_, ...), custom_call_target="tpu_custom_call" | custom-call | tf_op jit(solution)/shard_map/cond/branch_1_fun/pallas_call | solution.py:1072
  280.7 5.5 %branch_1_fun.17 = (f32[1,28,64,768]{3,2,1,0:T(8,128)}, f32[1,28,64,768]{3,2,1,0:T(8,128)}, f32[1,28,64,768]{3,2,1,0:T(8,128)}) custom-call(s32[105]{0:T(128)S(1)} %get-tuple-element.122.plan_ref, f32[1,28,64,768]{3,2,1,0:T(8,128)S(1)} %copy-done.1, ...), custom_call_target="tpu_custom_call", output_to_operand_aliasing={{0}: (8, {}), {1}: (9, {}), {2}: (10, {})} | custom-call | tf_op jit(solution)/shard_map/cond/branch_1_fun/pallas_call | solution.py:914
  286.4 42.4 %conditional.7 = (f32[1,28,64,768]{3,2,1,0:T(8,128)}, f32[1,28,64,768]{3,2,1,0:T(8,128)}, f32[1,28,64,768]{3,2,1,0:T(8,128)}, f32[8,768]{1,0:T(8,128)S(1)}) conditional(s32[]{:T(128)} %bitcast.25, () %tuple.46, (bf16[400,768]{1,0:T(8,128)(2,1)}, bf16[12,64,768]{2,1,0:T(8,128)(2,1)}, bf16[12,64,768]{2,1,0:T(8,128)(2,1)}, s32[105]{0:T(128)S(1)}, ...), branch_computations={%region_29.30_spmd, %region_30.31_spmd} | conditional | flops 1185792 | bytes 38314684 | solution.py:655
  292.3 4.6 %branch_1_fun.18 = (f32[1,28,64,768]{3,2,1,0:T(8,128)}, f32[1,28,64,768]{3,2,1,0:T(8,128)}, f32[1,28,64,768]{3,2,1,0:T(8,128)}) custom-call(s32[105]{0:T(128)S(1)} %get-tuple-element.138.plan_ref, f32[1,28,64,768]{3,2,1,0:T(8,128)} %get-tuple-element.134.refs_0_, ...), custom_call_target="tpu_custom_call", output_to_operand_aliasing={{0}: (8, {}), {1}: (9, {}), {2}: (10, {})} | custom-call | tf_op jit(solution)/shard_map/cond/branch_1_fun/pallas_call | solution.py:914
  314.1 5.3 %collective-permute-start.19 = (bf16[6,64,768]{2,1,0:T(8,128)(2,1)S(1)}, bf16[6,64,768]{2,1,0:T(8,128)(2,1)S(1)}, u32[]{:S(2)}, u32[]{:S(2)}) collective-permute-start(bf16[6,64,768]{2,1,0:T(8,128)(2,1)S(1)} %bitcast.52), channel_id=1, source_target_pairs={{0,4},{4,0},{8,12},{12,8},{16,20},{20,16},{24,28},{28,24},{1,5},{5... | collective-permute-start | bytes 1769480 | tf_op jit(solution)/shard_map/cond/branch_1_fun/ppermute | solution.py:625
  (232 shorter events, 124.5 us)
Async XLA Ops:
  7.2 62.4 %all-gather.4.cloned.1.call-start = ((), (), s32[]{:S(2)}) async-start(), calls=%async_computation.4 | async-start | bytes 3194880 | tf_op jit(solution)/shard_map/all_gather | solution.py:596
  13.4 19.4 %collective-permute-start.25 = (bf16[28,64,768]{2,1,0:T(8,128)(2,1)}, bf16[28,64,768]{2,1,0:T(8,128)(2,1)}, u32[]{:S(2)}, u32[]{:S(2)}) collective-permute-start(bf16[28,64,768]{2,1,0:T(8,128)(2,1)} %shard_map.222.refs_0_.refs_4_), channel_id=1, source_target_pairs={{0,4},{4,0},{8,12},{12,8},{16,20},{20,16},{24,28},{28,24},{1,5},{5... | collective-permute-start | bytes 8257544 | tf_op jit(solution)/shard_map/ppermute | solution.py:625
  13.5 98.6 %reduce-scatter.5.cloned.1.call-start = ((), (), s32[]{:S(2)}) async-start(), calls=%async_computation.5 | async-start | bytes 1597440 | tf_op jit(solution)/shard_map/reduce_scatter | solution.py:600
  24.2 59.9 %collective-permute-start.26 = (bf16[28,64,768]{2,1,0:T(8,128)(2,1)S(1)}, bf16[28,64,768]{2,1,0:T(8,128)(2,1)}, u32[]{:S(2)}, u32[]{:S(2)}) collective-permute-start(bf16[28,64,768]{2,1,0:T(8,128)(2,1)S(1)} %copy-done.2), channel_id=1, source_target_pairs={{0,8},{4,20},{8,0},{12,28},{16,24},{20,4},{24,16},{28,12},{1,9},{5... | collective-permute-start | bytes 8257544 | tf_op jit(solution)/shard_map/ppermute | solution.py:631
  32.9 64.3 %collective-permute-start.27 = (bf16[28,64,768]{2,1,0:T(8,128)(2,1)}, bf16[28,64,768]{2,1,0:T(8,128)(2,1)}, u32[]{:S(2)}, u32[]{:S(2)}) collective-permute-start(bf16[28,64,768]{2,1,0:T(8,128)(2,1)} %shard_map.228.refs_1_), channel_id=1, source_target_pairs={{0,8},{4,20},{8,0},{12,28},{16,24},{20,4},{24,16},{28,12},{1,9},{5... | collective-permute-start | bytes 8257544 | tf_op jit(solution)/shard_map/ppermute | solution.py:631
  34.4 15.5 %collective-permute-start.23 = (bf16[6,64,768]{2,1,0:T(8,128)(2,1)S(1)}, bf16[6,64,768]{2,1,0:T(8,128)(2,1)}, u32[]{:S(2)}, u32[]{:S(2)}) collective-permute-start(bf16[6,64,768]{2,1,0:T(8,128)(2,1)S(1)} %copy-done.6), channel_id=1, source_target_pairs={{0,16},{4,12},{8,24},{12,4},{16,0},{20,28},{24,8},{28,20},{1,17},{... | collective-permute-start | bytes 1769480 | tf_op jit(solution)/shard_map/ppermute | solution.py:631
  83.1 65.5 %all-gather.6.cloned.1.call-start = ((), (), s32[]{:S(2)}) async-start(), calls=%async_computation.6 | async-start | bytes 1597440 | tf_op jit(solution)/shard_map/all_gather | solution.py:596
  97.2 32.5 %collective-permute-start.28 = (bf16[28,64,768]{2,1,0:T(8,128)(2,1)}, bf16[28,64,768]{2,1,0:T(8,128)(2,1)}, u32[]{:S(2)}, u32[]{:S(2)}) collective-permute-start(bf16[28,64,768]{2,1,0:T(8,128)(2,1)} %shard_map.229.refs_2_), channel_id=1, source_target_pairs={{0,16},{4,12},{8,24},{12,4},{16,0},{20,28},{24,8},{28,20},{1,17},{... | collective-permute-start | bytes 8257544 | tf_op jit(solution)/shard_map/ppermute | solution.py:631
  98.9 36.0 %collective-permute-start.29 = (bf16[28,64,768]{2,1,0:T(8,128)(2,1)}, bf16[28,64,768]{2,1,0:T(8,128)(2,1)}, u32[]{:S(2)}, u32[]{:S(2)}) collective-permute-start(bf16[28,64,768]{2,1,0:T(8,128)(2,1)} %shard_map.229.refs_2_), channel_id=1, source_target_pairs={{0,4},{4,0},{8,12},{12,8},{16,20},{20,16},{24,28},{28,24},{1,5},{5... | collective-permute-start | bytes 8257544 | tf_op jit(solution)/shard_map/ppermute | solution.py:625
  100.6 39.6 %collective-permute-start.30 = (bf16[28,64,768]{2,1,0:T(8,128)(2,1)}, bf16[28,64,768]{2,1,0:T(8,128)(2,1)}, u32[]{:S(2)}, u32[]{:S(2)}) collective-permute-start(bf16[28,64,768]{2,1,0:T(8,128)(2,1)} %collective-permute-done.27.refs_1_.refs_3_), channel_id=1, source_target_pairs={{0,4},{4,0},{8,12},{12,8},{16,20},{20,16},{24,28},{28,24},{1,5},{5... | collective-permute-start | bytes 8257544 | tf_op jit(solution)/shard_map/ppermute | solution.py:625
  114.5 100.7 %reduce-scatter.7.cloned.1.call-start = ((), (), s32[]{:S(2)}) async-start(), calls=%async_computation.7 | async-start | bytes 1720320 | tf_op jit(solution)/shard_map/reduce_scatter | solution.py:600
  180.2 74.7 %all-gather.8.cloned.1.call-start = ((), (), s32[]{:S(2)}) async-start(), calls=%async_computation.8 | async-start | bytes 1597440 | tf_op jit(solution)/shard_map/all_gather | solution.py:596
  186.6 19.9 %collective-permute-start.7 = (bf16[12,64,768]{2,1,0:T(8,128)(2,1)}, bf16[12,64,768]{2,1,0:T(8,128)(2,1)S(1)}, u32[]{:S(2)}, u32[]{:S(2)}) collective-permute-start(bf16[12,64,768]{2,1,0:T(8,128)(2,1)} %fusion.refs_1_), channel_id=1, source_target_pairs={{0,16},{4,12},{8,24},{12,4},{16,0},{20,28},{24,8},{28,20},{1,17},{... | collective-permute-start | bytes 3538952 | tf_op jit(solution)/shard_map/cond/branch_1_fun/ppermute | solution.py:631
  194.7 20.5 %collective-permute-start.6 = (bf16[12,64,768]{2,1,0:T(8,128)(2,1)S(1)}, bf16[12,64,768]{2,1,0:T(8,128)(2,1)}, u32[]{:S(2)}, u32[]{:S(2)}) collective-permute-start(bf16[12,64,768]{2,1,0:T(8,128)(2,1)S(1)} %fusion.2), channel_id=1, source_target_pairs={{0,8},{4,20},{8,0},{12,28},{16,24},{20,4},{24,16},{28,12},{1,9},{5... | collective-permute-start | bytes 3538952 | tf_op jit(solution)/shard_map/cond/branch_1_fun/ppermute | solution.py:631
  219.0 67.3 %reduce-scatter.9.cloned.1.call-start = ((), (), s32[]{:S(2)}) async-start(), calls=%async_computation.9 | async-start | bytes 1597440 | tf_op jit(solution)/shard_map/reduce_scatter | solution.py:600
  219.6 110.5 %reduce-scatter.11.cloned.1.call-start = ((), (), s32[]{:S(2)}) async-start(), calls=%async_computation.10 | async-start | bytes 1597440 | tf_op jit(solution)/shard_map/reduce_scatter | solution.py:600
  219.7 16.0 %collective-permute-start.8 = (bf16[12,64,768]{2,1,0:T(8,128)(2,1)}, bf16[12,64,768]{2,1,0:T(8,128)(2,1)S(1)}, u32[]{:S(2)}, u32[]{:S(2)}) collective-permute-start(bf16[12,64,768]{2,1,0:T(8,128)(2,1)} %get-tuple-element.105), channel_id=1, source_target_pairs={{0,8},{4,20},{8,0},{12,28},{16,24},{20,4},{24,16},{28,12},{1,9},{5... | collective-permute-start | bytes 3538952 | tf_op jit(solution)/shard_map/cond/branch_1_fun/ppermute | solution.py:631
  221.4 14.2 %collective-permute-start.9 = (bf16[12,64,768]{2,1,0:T(8,128)(2,1)}, bf16[12,64,768]{2,1,0:T(8,128)(2,1)S(1)}, u32[]{:S(2)}, u32[]{:S(2)}) collective-permute-start(bf16[12,64,768]{2,1,0:T(8,128)(2,1)} %get-tuple-element.106), channel_id=1, source_target_pairs={{0,4},{4,0},{8,12},{12,8},{16,20},{20,16},{24,28},{28,24},{1,5},{5... | collective-permute-start | bytes 3538952 | tf_op jit(solution)/shard_map/cond/branch_1_fun/ppermute | solution.py:625
  239.2 15.7 %collective-permute-start.11 = (bf16[12,64,768]{2,1,0:T(8,128)(2,1)}, bf16[12,64,768]{2,1,0:T(8,128)(2,1)}, u32[]{:S(2)}, u32[]{:S(2)}) collective-permute-start(bf16[12,64,768]{2,1,0:T(8,128)(2,1)} %fusion.4), channel_id=1, source_target_pairs={{0,8},{4,20},{8,0},{12,28},{16,24},{20,4},{24,16},{28,12},{1,9},{5... | collective-permute-start | bytes 3538952 | tf_op jit(solution)/shard_map/cond/branch_1_fun/ppermute | solution.py:631
  240.7 14.2 %collective-permute-start.10 = (bf16[12,64,768]{2,1,0:T(8,128)(2,1)}, bf16[12,64,768]{2,1,0:T(8,128)(2,1)}, u32[]{:S(2)}, u32[]{:S(2)}) collective-permute-start(bf16[12,64,768]{2,1,0:T(8,128)(2,1)} %fusion.4), channel_id=1, source_target_pairs={{0,4},{4,0},{8,12},{12,8},{16,20},{20,16},{24,28},{28,24},{1,5},{5... | collective-permute-start | bytes 3538952 | tf_op jit(solution)/shard_map/cond/branch_1_fun/ppermute | solution.py:625
  254.9 25.9 %collective-permute-start.3 = (bf16[12,64,768]{2,1,0:T(8,128)(2,1)}, bf16[12,64,768]{2,1,0:T(8,128)(2,1)}, u32[]{:S(2)}, u32[]{:S(2)}) collective-permute-start(bf16[12,64,768]{2,1,0:T(8,128)(2,1)} %get-tuple-element.121.refs_5_), channel_id=1, source_target_pairs={{0,4},{4,0},{8,12},{12,8},{16,20},{20,16},{24,28},{28,24},{1,5},{5... | collective-permute-start | bytes 3538952 | tf_op jit(solution)/shard_map/cond/branch_1_fun/ppermute | solution.py:625
  256.6 29.7 %collective-permute-start.1 = (bf16[12,64,768]{2,1,0:T(8,128)(2,1)}, bf16[12,64,768]{2,1,0:T(8,128)(2,1)}, u32[]{:S(2)}, u32[]{:S(2)}) collective-permute-start(bf16[12,64,768]{2,1,0:T(8,128)(2,1)} %get-tuple-element.120.refs_4_), channel_id=1, source_target_pairs={{0,8},{4,20},{8,0},{12,28},{16,24},{20,4},{24,16},{28,12},{1,9},{5... | collective-permute-start | bytes 3538952 | tf_op jit(solution)/shard_map/cond/branch_1_fun/ppermute | solution.py:631
  258.0 28.3 %collective-permute-start.2 = (bf16[12,64,768]{2,1,0:T(8,128)(2,1)}, bf16[12,64,768]{2,1,0:T(8,128)(2,1)}, u32[]{:S(2)}, u32[]{:S(2)}) collective-permute-start(bf16[12,64,768]{2,1,0:T(8,128)(2,1)} %get-tuple-element.121.refs_5_), channel_id=1, source_target_pairs={{0,16},{4,12},{8,24},{12,4},{16,0},{20,28},{24,8},{28,20},{1,17},{... | collective-permute-start | bytes 3538952 | tf_op jit(solution)/shard_map/cond/branch_1_fun/ppermute | solution.py:631
  287.0 11.3 %collective-permute-start.12 = (bf16[400,768]{1,0:T(8,128)(2,1)}, bf16[400,768]{1,0:T(8,128)(2,1)S(1)}, u32[]{:S(2)}, u32[]{:S(2)}) collective-permute-start(bf16[400,768]{1,0:T(8,128)(2,1)} %get-tuple-element.137.left_ref), channel_id=1, source_target_pairs={{0,8},{4,20},{8,0},{12,28},{16,24},{20,4},{24,16},{28,12},{1,9},{5... | collective-permute-start | bytes 1843208 | tf_op jit(solution)/shard_map/cond/branch_1_fun/ppermute | solution.py:631
  (48 other events, 470.4 us)
Sparse Core Ops, SparseCore 0:
  13.6 55.8 all-gather.3
  83.2 28.9 reduce-scatter.4
  114.6 30.4 all-gather.5
  180.3 33.6 reduce-scatter.6
  219.1 32.7 all-gather.7
  254.1 30.1 reduce-scatter.8
  286.8 34.0 reduce-scatter.10

commit v2 on v1

--- a/solution.py
+++ b/solution.py
@@ -260,15 +260,36 @@
 
 
 def prepare_kernel(base, banks, table_ref, *refs):
-    bank, refs = refs[:banks], refs[banks:]
+    bank = refs[:banks]
     tiles_ref, semaphore = refs[-2:]
     count = tiles_ref.shape[0]
 
-    def start(source, tile):
-        pltpu.make_async_copy(source, tiles_ref.at[tile - base], semaphore).start()
-
-    fetch_tiles(table_ref, bank, base, base + count, start)
-    pltpu.make_async_copy(tiles_ref, tiles_ref, semaphore).wait()
+    def copy(source, tile):
+        return pltpu.make_async_copy(source, tiles_ref.at[tile - base], semaphore.at[tile - base])
+
+    fetch_tiles(table_ref, bank, base, base + count, lambda *a: copy(*a).start())
+    fetch_tiles(table_ref, bank, base, base + count, lambda *a: copy(*a).wait())
+
+
+def place_kernel(base, banks, table_ref, *refs):
+    bank = refs[:banks]
+    tiles_ref, held, read_semaphore, write_semaphore = refs[-4:]
+    count = tiles_ref.shape[0]
+
+    def read(source, tile):
+        return pltpu.make_async_copy(source, held.at[tile - base], read_semaphore.at[tile - base])
+
+    def write(_, tile):
+        place = tile - base
+        return pltpu.make_async_copy(held.at[place], tiles_ref.at[place], write_semaphore.at[place])
+
+    def settle(source, tile):
+        read(source, tile).wait()
+        write(source, tile).start()
+
+    fetch_tiles(table_ref, bank, base, base + count, lambda *a: read(*a).start())
+    fetch_tiles(table_ref, bank, base, base + count, settle)
+    fetch_tiles(table_ref, bank, base, base + count, lambda *a: write(*a).wait())
 
 
 def expert_kernel(images, runs, place_of_ref, *refs):
@@ -839,33 +860,6 @@
     mine = jnp.where(core == 0, ALONG_X, ALONG_Y)
     other = ALONG_X + ALONG_Y - mine
     far_away = ALONG_X + ALONG_Y
-    if paired:
-        first = after(first, [first_beside])
-        across = after(hop(first, second=True), [picked_grads])
-        far_pieces = [
-            (0, 0, slab),
-            (CORE, 0, slab_beside),
-            (mine, 0, first),
-            (mine + CORE, 0, first_beside),
-            (far_away, 0, across),
-            (other + CORE, 0, swap(first)),
-            (other, 0, swap(first_beside)),
-        ]
-        cuts = 4 if slot_width % 4 == 0 else 1
-        size = slot_width // cuts
-        far_pieces += [
-            (far_away + CORE, i, swap(across[i : i + size])) for i in range(0, slot_width, size)
-        ]
-        far_banks = [p for _, _, p in far_pieces]
-        far_table = jnp.concatenate(
-            [
-                lax.dynamic_index_in_dim(tile_at, r, 0, keepdims=False)[f : f + p.shape[0]]
-                for r, f, p in far_pieces
-            ]
-        )
-    else:
-        far_banks, far_table = near_banks, near_table
-
     near_here = slot_here[:near_tiles]
 
     def plan(wanted, table):
@@ -908,6 +902,20 @@
         plans = [after(plan(w, t), [second_rows]) for w, t in zip(wanted, tables)]
     else:
         plans = []
+
+    if paired:
+        def rows_of(*order):
+            return jnp.concatenate(
+                [lax.dynamic_index_in_dim(tile_at, r, 0, keepdims=False) for r in order]
+            )
+
+        far_table = rows_of(0, CORE, mine, mine + CORE, other + CORE, other)
+        last_table = rows_of(far_away, far_away + CORE)
+        first = after(first, [first_beside])
+        across = hop(first, second=True)
+        far_banks = [slab, slab_beside, first, first_beside, swap(first), swap(first_beside)]
+    else:
+        far_banks, far_table = near_banks, near_table
 
     def update(table, sources, olds):
         ahead, behind = 4, 3
@@ -949,15 +957,36 @@
     pieces_shape = (images * piece_shape[0], model)
     expert_tiles = (EXPERTS, 2 * runs, head, model)
 
+    tiles_shape_here = (far_tiles, head, model)
     tiles = call(
         functools.partial(prepare_kernel, near_tiles, len(far_banks)),
         (1,),
-        [any_spec] * (len(far_banks) + 1 + len(plans)),
-        whole((far_tiles, head, model)),
-        shaped((far_tiles, head, model), low_type),
-        scratch=[pltpu.SemaphoreType.DMA(())],
+        [any_spec] * (len(far_banks) + 1),
+        whole(tiles_shape_here),
+        shaped(tiles_shape_here, low_type),
+        scratch=[pltpu.SemaphoreType.DMA((far_tiles,))],
         prefetch=1,
-    )(far_table, *far_banks, second_rows, *plans)
+    )(far_table, *far_banks, second_rows)
+    if paired:
+        across = after(across, [picked_grads, last_table, router_rows, tiles, *plans])
+        across_swapped = region(flag, swap, across)
+        tiles = pl.pallas_call(
+            functools.partial(place_kernel, near_tiles, 2),
+            grid_spec=pltpu.PrefetchScalarGridSpec(
+                num_scalar_prefetch=1,
+                grid=(1,),
+                in_specs=[any_spec] * 3,
+                out_specs=any_spec,
+                scratch_shapes=[
+                    pltpu.VMEM(tiles_shape_here, low_type),
+                    pltpu.SemaphoreType.DMA((far_tiles,)),
+                    pltpu.SemaphoreType.DMA((far_tiles,)),
+                ],
+            ),
+            out_shape=shaped(tiles_shape_here, low_type),
+            input_output_aliases={3: 0},
+            compiler_params=pltpu.CompilerParams(vmem_limit_bytes=VMEM_BYTES),
+        )(last_table, across, across_swapped, tiles)
     sent_first, sent, kept, gated, pieces = call(
         functools.partial(expert_kernel, images, runs),
         (EXPERTS,),

time: 342 us -> 338 us (0.988)
  starting transfers between devices: 44.4 us -> 29.3 us
  waiting for transfers between devices: 103 us -> 116 us
    ppermute x18 -> x15, waiting for transfers between devices: 12 us -> 23.4 us  [swap(): return lax.ppermute(values, 'dp', [(i, i ^ CORE) for i in range(size)])]
    ppermute x18 -> x15, starting transfers between devices: 15.4 us -> 7.8 us  [swap(): return lax.ppermute(values, 'dp', [(i, i ^ CORE) for i in range(size)])]
    reduce_scatter x4, waiting for transfers between devices: 10.7 us -> 3.57 us  [scatter_rows(): return lax.psum_scatter(rows, 'tensor', scatter_dimension=0, tiled=True)]
    ppermute x14, starting transfers between devices: 23.5 us -> 16.5 us  [hop(): lax.ppermute(values, 'dp', [(i, i ^ along[i & CORE]) for i in range(size)])]
    ppermute x14, waiting for transfers between devices: 58.4 us -> 65.3 us  [hop(): lax.ppermute(values, 'dp', [(i, i ^ along[i & CORE]) for i in range(size)])]
    pallas_call x0 -> x1, Pallas kernels: none -> 4.63 us  [on_device(): pl.pallas_call(functools.partial(place_kernel, near_tiles, 2), grid_spec=...]
  transfers between devices with their start and end apart: 42 -> 39, of which waited for: 19 -> 21; matrix products, arithmetic and copies ran while one was open for 10% -> 9% of each run, Pallas kernels for 27% -> 30%
where the time goes in v2:
time: 338 us; the launch traced here: 337 us
  Pallas kernels  141 us (42%)
  waiting for transfers between devices  116 us (34%)
  starting transfers between devices  29.3 us (9%)
  other arithmetic  24.2 us (7%)
  between operations  14.5 us (4%)
  local copies, waits for them, and re-layouts  11.6 us (3%)
    ppermute x14, waiting for transfers between devices, hop(): lax.ppermute(values, 'dp', [(i, i ^ along[i & CORE]) for i in range(size)])  65.3 us
    pallas_call x1, Pallas kernels, on_device(): call(functools.partial(expert_kernel, images, runs), (EXPERTS,), [pl.Bloc...  31.6 us
    pallas_call x4, Pallas kernels, update(): pl.pallas_call(functools.partial(bank_kernel, len(sources)), grid_spec=pl...  23.9 us
    ppermute x15, waiting for transfers between devices, swap(): return lax.ppermute(values, 'dp', [(i, i ^ CORE) for i in range(size)])  23.4 us
    all_gather x3, waiting for transfers between devices, gather_rows(): return lax.all_gather(rows, 'tensor', axis=0, tiled=True)  18.9 us
    ppermute x14, starting transfers between devices, hop(): lax.ppermute(values, 'dp', [(i, i ^ along[i & CORE]) for i in range(size)])  16.5 us
    pallas_call x1, Pallas kernels, attend_back(): call(functools.partial(attend_back_kernel, images, heads, len(near_banks)...  15.9 us
    convert_element_type x8, other arithmetic, add_low(): return total.astype(low_type)  15.3 us
  transfers between devices with their start and end apart: 39, of which 21 were waited for; matrix products, arithmetic and copies ran while one was open for 9% of the time, Pallas kernels for 30%

profile of v2, /device:TPU:1, one launch (start us, length us, event | category | flops | bytes accessed | tf_op | source)
XLA Modules:
  0.0 337.2 jit_solution(7957988861380381853)
XLA Ops:
  9.7 3.8 %shard_map.222.refs_0_.refs_4_ = bf16[28,64,768]{2,1,0:T(8,128)(2,1)} custom-call(f32[1,28,64,768]{3,2,1,0:T(8,128)} %weight_ref.3, bf16[208,1536]{1,0:T(8,128)(2,1)} %shard_map.221.refs_0_), custom_call_target="tpu_custom_call" | custom-call | tf_op jit(solution)/shard_map/pallas_call | solution.py:771
  24.0 7.7 %collective-permute-done.23 = bf16[6,64,768]{2,1,0:T(8,128)(2,1)S(1)} collective-permute-done((bf16[6,64,768]{2,1,0:T(8,128)(2,1)S(1)}, bf16[6,64,768]{2,1,0:T(8,128)(2,1)S(1)}, u32[]{:S(2)}, u32[]{:S(2)}) %collective-permute-start.23) | collective-permute-done | bytes 589856 | tf_op jit(solution)/shard_map/ppermute | solution.py:652
  36.0 9.2 %shard_map.224 = (bf16[4,448,832]{2,1,0:T(8,128)(2,1)}, bf16[832,1792]{1,0:T(8,128)(2,1)}) custom-call(f32[832,2]{1,0:T(8,128)} %copy.63.col_ref, f32[2,832]{1,0:T(2,128)} %bitcast.54), custom_call_target="tpu_custom_call" | custom-call | tf_op jit(solution)/shard_map/pallas_call | solution.py:789
  46.6 18.9 %all-gather.4.cloned.1.call-done.refs_1_.refs_2_.cotangent_ref = bf16[832,1536]{1,0:T(8,128)(2,1)} async-done(((bf16[208,1536]{1,0:T(8,128)(2,1)}), bf16[832,1536]{1,0:T(8,128)(2,1)}) %all-gather.4.cloned.1.call-update) | async-done | bytes 2555920 | tf_op jit(solution)/shard_map/all_gather | solution.py:617
  68.0 10.9 %shard_map.226 = (bf16[832,768]{1,0:T(8,128)(2,1)}, bf16[4,208,576]{2,1,0:T(8,128)(2,1)}, bf16[4,208,192]{2,1,0:T(8,128)(2,1)}, bf16[832,768]{1,0:T(8,128)(2,1)}) custom-call(s32[12]{0:T(128)S(1)} %pad_add_fusion.table_ref, bf16[6,64,768]{2,1,0:T(8,128)(2,1)S(1)} %shard_map.225.refs_0_, bf16[6,64,768]{2,1,0:T(8,128)(2,1)} %collective-permute-done.25.refs_1_, ...), custom_call_target="tpu_custom_call" | custom-call | tf_op jit(solution)/shard_map/pallas_call | solution.py:836
  82.1 19.0 %collective-permute-done.28.refs_1_.refs_3_ = bf16[28,64,768]{2,1,0:T(8,128)(2,1)} collective-permute-done((bf16[28,64,768]{2,1,0:T(8,128)(2,1)}, bf16[28,64,768]{2,1,0:T(8,128)(2,1)}, u32[]{:S(2)}, u32[]{:S(2)}) %collective-permute-start.28) | collective-permute-done | bytes 2752544 | tf_op jit(solution)/shard_map/ppermute | solution.py:652
  117.3 6.1 %shard_map.230.refs_1_ = bf16[4,448,768]{2,1,0:T(8,128)(2,1)} custom-call(bf16[832,1536]{1,0:T(8,128)(2,1)S(1)} %copy-done.3, bf16[4,448,832]{2,1,0:T(8,128)(2,1)} %get-tuple-element.211.refs_2_.pick_ref.refs_4_, bf16[208,768]{1,0:T(8,128)(2,1)} %get-tuple-element.214._.refs_6_.refs_1_.second_ref), custom_call_target="tpu_custom_call" | custom-call | tf_op jit(solution)/shard_map/pallas_call | solution.py:852
  123.5 8.8 %shard_map.231.refs_4_.refs_2_ = bf16[96,64,768]{2,1,0:T(8,128)(2,1)} custom-call(s32[168]{0:T(256)} %concatenate.39.table_ref, bf16[28,64,768]{2,1,0:T(8,128)(2,1)} %shard_map.222.refs_0_.refs_4_, bf16[28,64,768]{2,1,0:T(8,128)(2,1)} %shard_map.228.refs_1_, bf16[28,64,768]{2,1,0:T(8,128)(2,1)} %shard_map.229.refs_2_, ...), custom_call_target="tpu_custom_call" | custom-call | tf_op jit(solution)/shard_map/pallas_call | solution.py:961
  133.7 6.4 %conditional.5 = (bf16[28,64,768]{2,1,0:T(8,128)(2,1)}) conditional(s32[]{:T(128)} %bitcast.24, () %tuple.46, bf16[28,64,768]{2,1,0:T(8,128)(2,1)} %shard_map.236.refs_0_), branch_computations={%region_20.21_spmd, %region_21.22_spmd} | conditional | bytes 11010096 | solution.py:676
  135.0 5.1 %collective-permute-done = bf16[28,64,768]{2,1,0:T(8,128)(2,1)} collective-permute-done((bf16[28,64,768]{2,1,0:T(8,128)(2,1)}, bf16[28,64,768]{2,1,0:T(8,128)(2,1)}, u32[]{:S(2)}, u32[]{:S(2)}) %collective-permute-start) | collective-permute-done | bytes 2752544 | tf_op jit(solution)/shard_map/cond/branch_1_fun/ppermute | solution.py:646
  140.1 4.6 %shard_map.237 = bf16[96,64,768]{2,1,0:T(8,128)(2,1)} custom-call(s32[56]{0:T(128)} %pad_add_fusion.1.refs_2_.table_ref, bf16[28,64,768]{2,1,0:T(8,128)(2,1)} %shard_map.236.refs_0_, bf16[28,64,768]{2,1,0:T(8,128)(2,1)} %get-tuple-element.329.refs_1_, bf16[96,64,768]{2,1,0:T(8,128)(2,1)} %shard_map.231.refs_4_.refs_2_), custom_call_target="tpu_custom_call", output_to_operand_aliasing={{}: (3, {})} | custom-call | tf_op jit(solution)/shard_map/pallas_call | solution.py:973
  144.8 31.6 %shard_map.238 = (bf16[12,64,768]{2,1,0:T(8,128)(2,1)}, bf16[3,12,64,768]{3,2,1,0:T(8,128)(2,1)}, bf16[4,12,64,768]{3,2,1,0:T(8,128)(2,1)}, bf16[4,448,768]{2,1,0:T(8,128)(2,1)}, bf16[896,768]{1,0:T(8,128)(2,1)}) custom-call(s32[8]{0:T(128)} %select_reduce_fusion.13.place_of_ref, bf16[4,24,64,768]{3,2,1,0:T(8,128)(2,1)} %bitcast.50, ...), custom_call_target="tpu_custom_call" | custom-call | tf_op jit(solution)/shard_map/pallas_call | solution.py:990
  176.4 34.8 %conditional.6 = (bf16[832,768]{1,0:T(8,128)(2,1)}, bf16[3,12,64,768]{3,2,1,0:T(8,128)(2,1)}, bf16[12,64,768]{2,1,0:T(8,128)(2,1)}, bf16[12,64,768]{2,1,0:T(8,128)(2,1)}) conditional(s32[]{:T(128)} %bitcast.24, () %tuple.47, (bf16[4,448,768]{2,1,0:T(8,128)(2,1)}, bf16[832,1792]{1,0:T(8,128)(2,1)}, bf16[4,12,64,768]{3,2,1,0:T(8,128)(2,1)}, ...), branch_computations={%region_23.24_spmd, %region_24.25_spmd} | conditional | flops 8257536 | bytes 52035804 | solution.py:676
  183.2 5.6 %collective-permute-done.6 = bf16[3,12,64,768]{3,2,1,0:T(8,128)(2,1)} collective-permute-done((bf16[3,12,64,768]{3,2,1,0:T(8,128)(2,1)}, bf16[3,12,64,768]{3,2,1,0:T(8,128)(2,1)}, u32[]{:S(2)}, u32[]{:S(2)}) %collective-permute-start.6) | collective-permute-done | bytes 3538976 | tf_op jit(solution)/shard_map/cond/branch_1_fun/ppermute | solution.py:646
  192.6 5.6 %branch_1_fun.12 = bf16[832,768]{1,0:T(8,128)(2,1)} custom-call(bf16[1792,768]{1,0:T(8,128)(2,1)} %bitcast.51, bf16[832,1792]{1,0:T(8,128)(2,1)S(1)} %copy-done.4), custom_call_target="tpu_custom_call" | custom-call | tf_op jit(solution)/shard_map/cond/branch_1_fun/pallas_call | solution.py:1030
  205.2 6.1 %collective-permute-done.7 = bf16[12,64,768]{2,1,0:T(8,128)(2,1)} collective-permute-done((bf16[12,64,768]{2,1,0:T(8,128)(2,1)S(1)}, bf16[12,64,768]{2,1,0:T(8,128)(2,1)}, u32[]{:S(2)}, u32[]{:S(2)}) %collective-permute-start.7) | collective-permute-done | bytes 1179680 | tf_op jit(solution)/shard_map/cond/branch_1_fun/ppermute | solution.py:652
  215.7 35.4 %conditional.7 = (f32[1,28,64,768]{3,2,1,0:T(8,128)}, f32[1,28,64,768]{3,2,1,0:T(8,128)}, f32[1,28,64,768]{3,2,1,0:T(8,128)}, bf16[12,64,768]{2,1,0:T(8,128)(2,1...) conditional(s32[]{:T(128)} %bitcast.24, () %tuple.50, (s32[57]{0:T(128)S(1)}, ...), branch_computations={%region_25.26_spmd, %region_26.27_spmd} | conditional | flops 4718592 | bytes 46792940 | solution.py:676
  217.8 14.2 %collective-permute-done.9 = bf16[12,64,768]{2,1,0:T(8,128)(2,1)S(1)} collective-permute-done((bf16[12,64,768]{2,1,0:T(8,128)(2,1)}, bf16[12,64,768]{2,1,0:T(8,128)(2,1)S(1)}, u32[]{:S(2)}, u32[]{:S(2)}) %collective-permute-start.9) | collective-permute-done | bytes 1179680 | tf_op jit(solution)/shard_map/cond/branch_1_fun/ppermute | solution.py:652
  238.1 13.0 %collective-permute-done.12 = bf16[12,64,768]{2,1,0:T(8,128)(2,1)} collective-permute-done((bf16[12,64,768]{2,1,0:T(8,128)(2,1)}, bf16[12,64,768]{2,1,0:T(8,128)(2,1)}, u32[]{:S(2)}, u32[]{:S(2)}) %collective-permute-start.12) | collective-permute-done | bytes 1179680 | tf_op jit(solution)/shard_map/cond/branch_1_fun/ppermute | solution.py:652
  251.1 35.3 %conditional.8 = (bf16[400,768]{1,0:T(8,128)(2,1)}, bf16[832,768]{1,0:T(8,128)(2,1)}, bf16[12,64,768]{2,1,0:T(8,128)(2,1)}, bf16[12,64,768]{2,1,0:T(8,128)(2,1)}...) conditional(s32[]{:T(128)} %bitcast.24, () %tuple.49, (s32[]{:T(128)}, ...), branch_computations={%region_27.28_spmd, %region_28.29_spmd} | conditional | bytes 41091344 | solution.py:676
  255.4 15.9 %branch_1_fun.15 = (bf16[400,768]{1,0:T(8,128)(2,1)}, bf16[400,768]{1,0:T(8,128)(2,1)}, bf16[832,768]{1,0:T(8,128)(2,1)}, f32[8,768]{1,0:T(8,128)}) custom-call(s32[12]{0:T(128)S(1)} %get-tuple-element.111.table_ref, s32[1]{0:T(128)} %bitcast.6.core_ref, bf16[6,64,768]{2,1,0:T(8,128)(2,1)} %get-tuple-element.113.refs_0_, ...), custom_call_target="tpu_custom_call" | custom-call | tf_op jit(solution)/shard_map/cond/branch_1_fun/pallas_call | solution.py:1101
  276.8 9.6 %branch_1_fun.17 = (f32[1,28,64,768]{3,2,1,0:T(8,128)}, f32[1,28,64,768]{3,2,1,0:T(8,128)}, f32[1,28,64,768]{3,2,1,0:T(8,128)}) custom-call(s32[105]{0:T(128)S(1)} %get-tuple-element.126.plan_ref, f32[1,28,64,768]{3,2,1,0:T(8,128)S(1)} %copy-done.1, ...), custom_call_target="tpu_custom_call", output_to_operand_aliasing={{0}: (8, {}), {1}: (9, {}), {2}: (10, {})} | custom-call | tf_op jit(solution)/shard_map/cond/branch_1_fun/pallas_call | solution.py:922
  286.6 39.3 %conditional.9 = (f32[1,28,64,768]{3,2,1,0:T(8,128)}, f32[1,28,64,768]{3,2,1,0:T(8,128)}, f32[1,28,64,768]{3,2,1,0:T(8,128)}, f32[8,768]{1,0:T(8,128)S(1)}) conditional(s32[]{:T(128)} %bitcast.24, () %tuple.53, (bf16[400,768]{1,0:T(8,128)(2,1)}, bf16[12,64,768]{2,1,0:T(8,128)(2,1)}, bf16[12,64,768]{2,1,0:T(8,128)(2,1)}, s32[105]{0:T(128)S(1)}, ...), branch_computations={%region_31.32_spmd, %region_32.33_spmd} | conditional | flops 1185792 | bytes 38314684 | solution.py:676
  292.5 9.6 %branch_1_fun.18 = (f32[1,28,64,768]{3,2,1,0:T(8,128)}, f32[1,28,64,768]{3,2,1,0:T(8,128)}, f32[1,28,64,768]{3,2,1,0:T(8,128)}) custom-call(s32[105]{0:T(128)S(1)} %get-tuple-element.142.plan_ref, f32[1,28,64,768]{3,2,1,0:T(8,128)} %get-tuple-element.138.refs_0_, ...), custom_call_target="tpu_custom_call", output_to_operand_aliasing={{0}: (8, {}), {1}: (9, {}), {2}: (10, {})} | custom-call | tf_op jit(solution)/shard_map/cond/branch_1_fun/pallas_call | solution.py:922
  (227 shorter events, 116.8 us)
Async XLA Ops:
  7.2 58.3 %all-gather.4.cloned.1.call-start = ((), (), s32[]{:S(2)}) async-start(), calls=%async_computation.4 | async-start | bytes 3194880 | tf_op jit(solution)/shard_map/all_gather | solution.py:617
  9.6 98.5 %reduce-scatter.5.cloned.1.call-start = ((), (), s32[]{:S(2)}) async-start(), calls=%async_computation.5 | async-start | bytes 1597440 | tf_op jit(solution)/shard_map/reduce_scatter | solution.py:621
  13.5 21.1 %collective-permute-start.27 = (bf16[28,64,768]{2,1,0:T(8,128)(2,1)}, bf16[28,64,768]{2,1,0:T(8,128)(2,1)}, u32[]{:S(2)}, u32[]{:S(2)}) collective-permute-start(bf16[28,64,768]{2,1,0:T(8,128)(2,1)} %shard_map.222.refs_0_.refs_4_), channel_id=1, source_target_pairs={{0,4},{4,0},{8,12},{12,8},{16,20},{20,16},{24,28},{28,24},{1,5},{5... | collective-permute-start | bytes 8257544 | tf_op jit(solution)/shard_map/ppermute | solution.py:646
  31.9 13.3 %collective-permute-start.24 = (bf16[6,64,768]{2,1,0:T(8,128)(2,1)S(1)}, bf16[6,64,768]{2,1,0:T(8,128)(2,1)}, u32[]{:S(2)}, u32[]{:S(2)}) collective-permute-start(bf16[6,64,768]{2,1,0:T(8,128)(2,1)S(1)} %add_convert_fusion.3.refs_1_), channel_id=1, source_target_pairs={{0,16},{4,12},{8,24},{12,4},{16,0},{20,28},{24,8},{28,20},{1,17},{... | collective-permute-start | bytes 1769480 | tf_op jit(solution)/shard_map/ppermute | solution.py:652
  33.4 48.7 %collective-permute-start.26 = (bf16[28,64,768]{2,1,0:T(8,128)(2,1)S(1)}, bf16[28,64,768]{2,1,0:T(8,128)(2,1)}, u32[]{:S(2)}, u32[]{:S(2)}) collective-permute-start(bf16[28,64,768]{2,1,0:T(8,128)(2,1)S(1)} %copy-done.2), channel_id=1, source_target_pairs={{0,8},{4,20},{8,0},{12,28},{16,24},{20,4},{24,16},{28,12},{1,9},{5... | collective-permute-start | bytes 8257544 | tf_op jit(solution)/shard_map/ppermute | solution.py:652
  34.6 66.5 %collective-permute-start.28 = (bf16[28,64,768]{2,1,0:T(8,128)(2,1)}, bf16[28,64,768]{2,1,0:T(8,128)(2,1)}, u32[]{:S(2)}, u32[]{:S(2)}) collective-permute-start(bf16[28,64,768]{2,1,0:T(8,128)(2,1)} %shard_map.228.refs_1_), channel_id=1, source_target_pairs={{0,8},{4,20},{8,0},{12,28},{16,24},{20,4},{24,16},{28,12},{1,9},{5... | collective-permute-start | bytes 8257544 | tf_op jit(solution)/shard_map/ppermute | solution.py:652
  78.9 65.8 %all-gather.6.cloned.1.call-start = ((), (), s32[]{:S(2)}) async-start(), calls=%async_computation.6 | async-start | bytes 1597440 | tf_op jit(solution)/shard_map/all_gather | solution.py:617
  101.1 22.3 %collective-permute-start.30 = (bf16[28,64,768]{2,1,0:T(8,128)(2,1)}, bf16[28,64,768]{2,1,0:T(8,128)(2,1)}, u32[]{:S(2)}, u32[]{:S(2)}) collective-permute-start(bf16[28,64,768]{2,1,0:T(8,128)(2,1)} %shard_map.229.refs_2_), channel_id=1, source_target_pairs={{0,4},{4,0},{8,12},{12,8},{16,20},{20,16},{24,28},{28,24},{1,5},{5... | collective-permute-start | bytes 8257544 | tf_op jit(solution)/shard_map/ppermute | solution.py:646
  101.1 32.5 %collective-permute-start.29 = (bf16[28,64,768]{2,1,0:T(8,128)(2,1)}, bf16[28,64,768]{2,1,0:T(8,128)(2,1)}, u32[]{:S(2)}, u32[]{:S(2)}) collective-permute-start(bf16[28,64,768]{2,1,0:T(8,128)(2,1)} %shard_map.229.refs_2_), channel_id=1, source_target_pairs={{0,16},{4,12},{8,24},{12,4},{16,0},{20,28},{24,8},{28,20},{1,17},{... | collective-permute-start | bytes 8257544 | tf_op jit(solution)/shard_map/ppermute | solution.py:652
  101.9 21.6 %collective-permute-start.31 = (bf16[28,64,768]{2,1,0:T(8,128)(2,1)}, bf16[28,64,768]{2,1,0:T(8,128)(2,1)}, u32[]{:S(2)}, u32[]{:S(2)}) collective-permute-start(bf16[28,64,768]{2,1,0:T(8,128)(2,1)} %collective-permute-done.28.refs_1_.refs_3_), channel_id=1, source_target_pairs={{0,4},{4,0},{8,12},{12,8},{16,20},{20,16},{24,28},{28,24},{1,5},{5... | collective-permute-start | bytes 8257544 | tf_op jit(solution)/shard_map/ppermute | solution.py:646
  110.4 100.8 %reduce-scatter.7.cloned.1.call-start = ((), (), s32[]{:S(2)}) async-start(), calls=%async_computation.7 | async-start | bytes 1720320 | tf_op jit(solution)/shard_map/reduce_scatter | solution.py:621
  176.4 74.8 %all-gather.8.cloned.1.call-start = ((), (), s32[]{:S(2)}) async-start(), calls=%async_computation.8 | async-start | bytes 1597440 | tf_op jit(solution)/shard_map/all_gather | solution.py:617
  182.6 19.4 %collective-permute-start.8 = (bf16[12,64,768]{2,1,0:T(8,128)(2,1)}, bf16[12,64,768]{2,1,0:T(8,128)(2,1)S(1)}, u32[]{:S(2)}, u32[]{:S(2)}) collective-permute-start(bf16[12,64,768]{2,1,0:T(8,128)(2,1)} %fusion.refs_1_), channel_id=1, source_target_pairs={{0,16},{4,12},{8,24},{12,4},{16,0},{20,28},{24,8},{28,20},{1,17},{... | collective-permute-start | bytes 3538952 | tf_op jit(solution)/shard_map/cond/branch_1_fun/ppermute | solution.py:652
  190.8 20.5 %collective-permute-start.7 = (bf16[12,64,768]{2,1,0:T(8,128)(2,1)S(1)}, bf16[12,64,768]{2,1,0:T(8,128)(2,1)}, u32[]{:S(2)}, u32[]{:S(2)}) collective-permute-start(bf16[12,64,768]{2,1,0:T(8,128)(2,1)S(1)} %fusion.2), channel_id=1, source_target_pairs={{0,8},{4,20},{8,0},{12,28},{16,24},{20,4},{24,16},{28,12},{1,9},{5... | collective-permute-start | bytes 3538952 | tf_op jit(solution)/shard_map/cond/branch_1_fun/ppermute | solution.py:652
  215.1 71.4 %reduce-scatter.9.cloned.1.call-start = ((), (), s32[]{:S(2)}) async-start(), calls=%async_computation.9 | async-start | bytes 1597440 | tf_op jit(solution)/shard_map/reduce_scatter | solution.py:621
  215.7 111.5 %reduce-scatter.11.cloned.1.call-start = ((), (), s32[]{:S(2)}) async-start(), calls=%async_computation.10 | async-start | bytes 1597440 | tf_op jit(solution)/shard_map/reduce_scatter | solution.py:621
  216.0 16.0 %collective-permute-start.9 = (bf16[12,64,768]{2,1,0:T(8,128)(2,1)}, bf16[12,64,768]{2,1,0:T(8,128)(2,1)S(1)}, u32[]{:S(2)}, u32[]{:S(2)}) collective-permute-start(bf16[12,64,768]{2,1,0:T(8,128)(2,1)} %get-tuple-element.109), channel_id=1, source_target_pairs={{0,8},{4,20},{8,0},{12,28},{16,24},{20,4},{24,16},{28,12},{1,9},{5... | collective-permute-start | bytes 3538952 | tf_op jit(solution)/shard_map/cond/branch_1_fun/ppermute | solution.py:652
  217.8 14.2 %collective-permute-start.10 = (bf16[12,64,768]{2,1,0:T(8,128)(2,1)}, bf16[12,64,768]{2,1,0:T(8,128)(2,1)S(1)}, u32[]{:S(2)}, u32[]{:S(2)}) collective-permute-start(bf16[12,64,768]{2,1,0:T(8,128)(2,1)} %get-tuple-element.110), channel_id=1, source_target_pairs={{0,4},{4,0},{8,12},{12,8},{16,20},{20,16},{24,28},{28,24},{1,5},{5... | collective-permute-start | bytes 3538952 | tf_op jit(solution)/shard_map/cond/branch_1_fun/ppermute | solution.py:646
  235.5 15.7 %collective-permute-start.12 = (bf16[12,64,768]{2,1,0:T(8,128)(2,1)}, bf16[12,64,768]{2,1,0:T(8,128)(2,1)}, u32[]{:S(2)}, u32[]{:S(2)}) collective-permute-start(bf16[12,64,768]{2,1,0:T(8,128)(2,1)} %fusion.4), channel_id=1, source_target_pairs={{0,8},{4,20},{8,0},{12,28},{16,24},{20,4},{24,16},{28,12},{1,9},{5... | collective-permute-start | bytes 3538952 | tf_op jit(solution)/shard_map/cond/branch_1_fun/ppermute | solution.py:652
  236.9 14.2 %collective-permute-start.11 = (bf16[12,64,768]{2,1,0:T(8,128)(2,1)}, bf16[12,64,768]{2,1,0:T(8,128)(2,1)}, u32[]{:S(2)}, u32[]{:S(2)}) collective-permute-start(bf16[12,64,768]{2,1,0:T(8,128)(2,1)} %fusion.4), channel_id=1, source_target_pairs={{0,4},{4,0},{8,12},{12,8},{16,20},{20,16},{24,28},{28,24},{1,5},{5... | collective-permute-start | bytes 3538952 | tf_op jit(solution)/shard_map/cond/branch_1_fun/ppermute | solution.py:646
  251.1 25.7 %collective-permute-start.4 = (bf16[12,64,768]{2,1,0:T(8,128)(2,1)}, bf16[12,64,768]{2,1,0:T(8,128)(2,1)}, u32[]{:S(2)}, u32[]{:S(2)}) collective-permute-start(bf16[12,64,768]{2,1,0:T(8,128)(2,1)} %get-tuple-element.125.refs_5_), channel_id=1, source_target_pairs={{0,4},{4,0},{8,12},{12,8},{16,20},{20,16},{24,28},{28,24},{1,5},{5... | collective-permute-start | bytes 3538952 | tf_op jit(solution)/shard_map/cond/branch_1_fun/ppermute | solution.py:646
  252.5 33.9 %collective-permute-start.2 = (bf16[12,64,768]{2,1,0:T(8,128)(2,1)}, bf16[12,64,768]{2,1,0:T(8,128)(2,1)}, u32[]{:S(2)}, u32[]{:S(2)}) collective-permute-start(bf16[12,64,768]{2,1,0:T(8,128)(2,1)} %get-tuple-element.124.refs_4_), channel_id=1, source_target_pairs={{0,8},{4,20},{8,0},{12,28},{16,24},{20,4},{24,16},{28,12},{1,9},{5... | collective-permute-start | bytes 3538952 | tf_op jit(solution)/shard_map/cond/branch_1_fun/ppermute | solution.py:652
  254.3 32.2 %collective-permute-start.3 = (bf16[12,64,768]{2,1,0:T(8,128)(2,1)}, bf16[12,64,768]{2,1,0:T(8,128)(2,1)}, u32[]{:S(2)}, u32[]{:S(2)}) collective-permute-start(bf16[12,64,768]{2,1,0:T(8,128)(2,1)} %get-tuple-element.125.refs_5_), channel_id=1, source_target_pairs={{0,16},{4,12},{8,24},{12,4},{16,0},{20,28},{24,8},{28,20},{1,17},{... | collective-permute-start | bytes 3538952 | tf_op jit(solution)/shard_map/cond/branch_1_fun/ppermute | solution.py:652
  287.2 14.8 %collective-permute-start.13 = (bf16[400,768]{1,0:T(8,128)(2,1)}, bf16[400,768]{1,0:T(8,128)(2,1)S(1)}, u32[]{:S(2)}, u32[]{:S(2)}) collective-permute-start(bf16[400,768]{1,0:T(8,128)(2,1)} %get-tuple-element.141.left_ref), channel_id=1, source_target_pairs={{0,8},{4,20},{8,0},{12,28},{16,24},{20,4},{24,16},{28,12},{1,9},{5... | collective-permute-start | bytes 1843208 | tf_op jit(solution)/shard_map/cond/branch_1_fun/ppermute | solution.py:652
  (45 other events, 423.2 us)
Sparse Core Ops, SparseCore 0:
  9.7 55.7 all-gather.3
  79.1 29.0 reduce-scatter.4
  110.6 30.6 all-gather.5
  176.5 33.4 reduce-scatter.6
  215.2 32.6 all-gather.7
  250.1 30.2 reduce-scatter.8
  286.7 30.9 reduce-scatter.10
